TPU v7x, 512 devices: a whole 4x4x16 slice. The times are simulated.
512 devices in a mesh: section: 4 (over z_hi), vocab: 32 (over z_lo, y, core), dp: 4 (over x).
Axes of the slice: x: 4, y: 4, z: 16 (z_hi: 4, z_lo: 4; z = z_hi * 4 + z_lo), core: 2. Of those that a mesh axis runs over, the one named last changes fastest.
Arguments:
- features: bfloat16 [4, 128, 32, 3072], P('dp', 'vocab', None, 'section'), may hold values from -6 to 6
- dw_weight: float32 [7, 7, 3072], P(None, None, 'section'), may hold values from -1.75 to 1.75
- ln_gain: float32 [3072], P('section'), may hold values from 0.25 to 1.75
- ln_bias: float32 [3072], P('section'), may hold values from -3 to 3
- layer_scale: float32 [3072], P('section'), may hold values from 0.25 to 2
- proj_weight: bfloat16 [3072, 8192], P('section', 'vocab'), may hold values from -0.109375 to 0.109375
- text_embed: bfloat16 [4, 512, 8192], P('dp', 'section', 'vocab'), may hold values from -6 to 6
- positions: int32 [4, 256], P('dp'), may hold values from 0 to 511, as said below
- rms_gain: float32 [8192], replicated, may hold values from 0.25 to 1.75
- head_weight: bfloat16 [8192, 64128], P('dp', ('section', 'vocab'))
- labels: int32 [4, 512], P('dp'), may hold values from 0 to 64127
Outputs:
- visual: bfloat16 [4, 256, 3072], P('dp', 'vocab', 'section')
- loss: float32 [4, 512], P('dp', 'section')
Inputs may be any that keep to these rules, and one draw needn't show every extreme that they name: The positions of one sequence are distinct.
All inputs are finite; a program needn't handle non-finite values.
Results may differ from a plain program's by a relative error of at most 0.008.
Values may be sent and summed in bfloat16 or wider, within the bound.
No kernel may reach another device: no remote copies, remote signals or barrier semaphores. Data moves between devices by JAX's collectives and lax.ppermute only.
A program may use at most 64 MiB of HBM per device.

v0:
```python
import functools

import jax
import jax.numpy as jnp
from jax import lax
from jax.experimental import pallas as pl
from jax.experimental.pallas import tpu as pltpu
from jax.sharding import PartitionSpec as P

WIDE = 256
VOCAB = ("zl", "y", "core")


def shifted(value, axis, step):
    count = lax.axis_size(axis)
    return lax.ppermute(value, axis, [((i + step) % count, i) for i in range(count)])


def extended(cells, axis, width):
    count = lax.axis_size(axis)
    ends = count - 1
    head, tail = cells[:width], cells[-width:]
    return jnp.concatenate(
        [
            lax.ppermute(tail, axis, [(i, (i + 1) % count) for i in range(ends)]),
            cells,
            lax.ppermute(head, axis, [((i + 1) % count, i) for i in range(ends)]),
        ],
        axis=0,
    )


def head_kernel(columns, offsets, from_text, own_ref, gain_ref, meta_ref, *refs):
    x_v, w_v, scaled, total, squares, sem_x, sem_w = refs[-7:]
    out_ref = refs[-8]
    w_low, w_own, w_left, w_right, w_far, w_off = refs[-14:-8]
    parts, lines, cores, rows, width = x_v.shape
    own, core = own_ref[0], own_ref[1]

    def block(j):
        return lax.rem(own + offsets[j], parts)

    def x_copies(j):
        if from_text:
            return [pltpu.make_async_copy(refs[0].at[block(j)], x_v.at[j], sem_x.at[j, 0])]
        return [
            pltpu.make_async_copy(
                refs[k].at[:, block(j)],
                x_v.at[j, :, core if k == 0 else 1 - core],
                sem_x.at[j, k],
            )
            for k in range(2)
        ]

    def w_copies(j):
        copies = [
            pltpu.make_async_copy(
                w_low.at[block(j)], w_v.at[j, pl.ds(0, WIDE)], sem_w.at[j, 0]
            )
        ]
        if j < 3:
            pieces = ((w_own, w_left, w_right)[j],)
        else:
            pieces = (w_far, w_off)
        size = WIDE // len(pieces)
        for k, piece in enumerate(pieces):
            copies.append(
                pltpu.make_async_copy(
                    piece, w_v.at[j, pl.ds(WIDE + k * size, size)], sem_w.at[j, k + 1]
                )
            )
        return copies

    for j in range(parts):
        for copy in x_copies(j) + w_copies(j):
            copy.start()
    for j in range(parts):
        for copy in x_copies(j):
            copy.wait()
        sums = jnp.zeros((rows, width), jnp.float32)
        for line in range(lines):
            for at in range(cores):
                piece = line * cores + at
                wide = x_v[j, line, at].astype(jnp.float32)
                sums = sums + wide * wide
                gain = gain_ref[block(j) * (lines * cores) + piece]
                scaled[:, piece * width : (piece + 1) * width] = (wide * gain).astype(
                    jnp.bfloat16
                )
        for copy in w_copies(j):
            copy.wait()
        part = lax.dot_general(
            scaled[...], w_v[j], (((1,), (1,)), ((), ())), preferred_element_type=jnp.float32
        )
        sums = jnp.sum(sums, axis=1, keepdims=True)
        if j == 0:
            total[...] = part
            squares[...] = sums
        else:
            total[...] += part
            squares[...] += sums
    factor = lax.rsqrt(squares[...] / (parts * lines * cores * width) + 1e-05)
    logits = total[...] * factor
    at = lax.broadcasted_iota(jnp.int32, logits.shape, 1)
    real = at < columns
    top = jnp.max(jnp.where(real, logits, -jnp.inf), axis=1, keepdims=True)
    summed = jnp.sum(
        jnp.where(real, jnp.exp(logits - top), 0.0), axis=1, keepdims=True
    )
    chosen = jnp.sum(
        jnp.where((at == meta_ref[:, 1:2]) & real, logits, 0.0), axis=1, keepdims=True
    )
    hit = (
        lax.broadcasted_iota(jnp.int32, (rows, out_ref.shape[1]), 1) == meta_ref[:, 0:1]
    )
    out_ref[...] = jnp.zeros(out_ref.shape, jnp.float32)
    for k, value in enumerate((top, summed, chosen)):
        out_ref[k : k + 1, :] = jnp.sum(jnp.where(hit, value, 0.0), axis=0, keepdims=True)


def head_stats(own, gain, meta, xs, weights, dep, columns, offsets, places):
    from_text = len(xs) == 1
    rows = meta.shape[0]
    parts, lines, cores = len(offsets), 4, 2
    width = xs[0].shape[-1]
    depth = lines * cores * width
    vmem = pl.BlockSpec(memory_space=pltpu.VMEM)
    anywhere = pl.BlockSpec(memory_space=pl.ANY)
    return pl.pallas_call(
        functools.partial(head_kernel, columns, offsets, from_text),
        out_shape=jax.ShapeDtypeStruct((8, places), jnp.float32),
        in_specs=[pl.BlockSpec(memory_space=pltpu.SMEM), vmem, vmem]
        + [anywhere] * (len(xs) + len(dep) + len(weights)),
        out_specs=vmem,
        scratch_shapes=[
            pltpu.VMEM((parts, lines, cores, rows, width), jnp.bfloat16),
            pltpu.VMEM((parts, 2 * WIDE, depth), jnp.bfloat16),
            pltpu.VMEM((rows, depth), jnp.bfloat16),
            pltpu.VMEM((rows, 2 * WIDE), jnp.float32),
            pltpu.VMEM((rows, 1), jnp.float32),
            pltpu.SemaphoreType.DMA((parts, 2)),
            pltpu.SemaphoreType.DMA((parts, 3)),
        ],
        compiler_params=pltpu.CompilerParams(vmem_limit_bytes=56 * 1024 * 1024),
        cost_estimate=pl.CostEstimate(
            flops=4 * rows * WIDE * parts * depth,
            bytes_accessed=2 * parts * depth * (rows + 2 * WIDE),
            transcendentals=2 * rows * WIDE,
        ),
    )(own, gain, meta, *xs, *dep, *weights)


def across(value, turn):
    count = lax.axis_size("section")
    pairs = [(i, i ^ 1) if turn == 0 else (i, count - 1 - i) for i in range(count)]
    return lax.ppermute(value, "section", pairs)


def to_all(value, axis):
    count = lax.axis_size(axis)
    return lax.all_to_all(jnp.broadcast_to(value[None], (count,) + value.shape), axis, 0, 0)


def shards(
    features,
    dw_weight,
    ln_gain,
    ln_bias,
    layer_scale,
    proj_weight,
    text_embed,
    positions,
    rms_gain,
    head_weight,
    labels,
):
    sections = lax.axis_size("section")
    parts = lax.axis_size("dp")
    shard_index = lax.axis_index(("section",) + VOCAB)
    places = positions[0]
    targets = labels[0]
    columns = head_weight.shape[1]
    slots = lax.iota(jnp.int32, targets.shape[0])

    text = to_all(text_embed[0], "section").reshape(slots.shape[0], -1)

    weight = head_weight.T
    low_all = lax.all_gather(weight[:WIDE], "dp", axis=0)
    high = jnp.pad(weight[WIDE:], ((0, 2 * WIDE - columns), (0, 0)))
    left, right = shifted(high, "dp", -1), shifted(high, "dp", 1)

    image = features[0]
    height, width, chans = image.shape
    padded = extended(image, VOCAB, 3)
    padded = jnp.pad(padded, ((0, 0), (3, 3), (0, 0))).astype(jnp.float32)
    conv = jnp.zeros((height, width, chans), jnp.float32)
    for row_off in range(7):
        for col_off in range(7):
            conv = (
                conv
                + padded[row_off : row_off + height, col_off : col_off + width]
                * dw_weight[row_off, col_off]
            )
    sums = jnp.stack(
        [jnp.sum(conv, axis=-1).reshape(-1), jnp.sum(conv * conv, axis=-1).reshape(-1)]
    )
    is_text = jnp.all(slots[:, None] != places[None, :], axis=1)
    rank = jnp.sum(
        jnp.where((slots[None, :] < slots[:, None]) & is_text[None, :], 1, 0), axis=1
    )
    text_rows = slots.shape[0] - places.shape[0]
    select = (rank[None, :] == lax.iota(jnp.int32, text_rows)[:, None]) & is_text[None, :]
    text, _ = lax.optimization_barrier((text, sums))
    text = jnp.dot(
        select.astype(jnp.bfloat16), text, preferred_element_type=jnp.float32
    ).astype(jnp.bfloat16)
    text_slots = jnp.sum(jnp.where(select, slots[None, :], 0), axis=1)
    text_all = lax.all_gather(text, VOCAB, axis=0)
    text_all = text_all.reshape(tuple(lax.axis_size(axis) for axis in VOCAB) + text.shape)
    sums = lax.psum(sums, "section")
    all_chans = chans * sections
    middle = sums[0].reshape(height, width) / all_chans
    spread = sums[1].reshape(height, width) / all_chans - middle * middle
    normal = (conv - middle[..., None]) * lax.rsqrt(spread + 1e-06)[..., None] * ln_gain + ln_bias
    block = image.astype(jnp.float32) + layer_scale * normal
    pooled = block.reshape(height // 4, 4, width // 4, 4, chans).mean(axis=(1, 3))
    pooled = pooled.reshape(-1, chans).astype(jnp.bfloat16)

    tokens = to_all(pooled, VOCAB).reshape(-1, chans)
    rows = jnp.dot(tokens, proj_weight, preferred_element_type=jnp.float32)
    for turn in range(2):
        rows = rows + across(rows.astype(jnp.bfloat16), turn).astype(jnp.float32)
    rows = rows.astype(jnp.bfloat16)

    rows, left, right = lax.optimization_barrier((rows, left, right))
    half = WIDE // 2
    far, off = shifted(left[:half], "dp", -1), shifted(right[half:], "dp", 1)
    rows = to_all(rows, "zl")
    rows, text_all, far, off = lax.optimization_barrier((rows, text_all, far, off))
    early = rows[0, :16, :128]
    rows = to_all(rows, "y")
    partner = lax.ppermute(rows, "core", [(0, 1), (1, 0)])

    gain = rms_gain.reshape(-1, 1, text.shape[1])
    own = jnp.stack([lax.axis_index("dp"), lax.axis_index("core")])
    offsets = (0, parts - 1, 1, 2)

    def stats(at, xs, dep):
        ids = jnp.sum(jnp.where(at[:, None] == slots[None, :], targets[None, :], 0), axis=1)
        ids = ids - shard_index * columns
        return head_stats(
            own,
            gain,
            jnp.stack([at, ids], axis=1),
            xs,
            (low_all, high, left, right, far, off),
            dep,
            columns,
            offsets,
            targets.shape[0],
        )

    of_text = stats(text_slots, (text_all,), (early,))
    of_visual = stats(places, (rows, partner), ())
    both = (of_text + of_visual)[:3]

    def merged(pieces):
        tops, totals, chosen = pieces[:, 0], pieces[:, 1], pieces[:, 2]
        top = jnp.max(tops, axis=0)
        return jnp.stack(
            [top, jnp.sum(totals * jnp.exp(tops - top), axis=0), jnp.sum(chosen, axis=0)]
        )

    for turn in range(2):
        both = merged(jnp.stack([both, across(both, turn)]))
    both = both.reshape(3, sections, -1)
    both = lax.dynamic_index_in_dim(both, lax.axis_index("section"), 1, keepdims=False)
    top, total, chosen = merged(to_all(both, VOCAB))
    loss = top + jnp.log(total) - chosen
    return (pooled[None], loss[None])


def solution(mesh):
    in_specs = (
        P("dp", VOCAB, None, "section"),
        P(None, None, "section"),
        P("section"),
        P("section"),
        P("section"),
        P("section", VOCAB),
        P("dp", "section", VOCAB),
        P("dp", None),
        P(),
        P("dp", ("section",) + VOCAB),
        P("dp", None),
    )
    out_specs = (P("dp", VOCAB, "section"), P("dp", "section"))
    sizes = (mesh.shape["section"], mesh.shape["vocab"] // 8, 4, 2, mesh.shape["dp"])
    mesh = jax.sharding.Mesh(mesh.devices.reshape(sizes), ("section",) + VOCAB + ("dp",))
    return jax.shard_map(shards, mesh=mesh, in_specs=in_specs, out_specs=out_specs, check_vma=False)
```

profile of v0, /device:TPU:1, one launch (start us, length us, event | category | flops | bytes accessed | tf_op | source)
XLA Modules:
  0.0 246.1 jit_solution(15196178513635631266)
XLA Ops:
  8.8 15.6 %all-to-all-start.2 = ((bf16[4,128,256]{2,1,0:T(8,128)(2,1)}), bf16[4,128,256]{2,1,0:T(8,128)(2,1)S(1)}, u32[]{:S(2)}, u32[]{:S(2)}) async-start(bf16[4,128,256]{2,1,0:T(8,128)(2,1)} %broadcast_in_dim.100), calls=%async_computation.2 | async-start | bytes 524288 | tf_op jit(solution)/shard_map/all_to_all | solution.py:161
  25.5 4.0 %collective-permute-start = (bf16[3,32,768]{2,1,0:T(8,128)(2,1)S(1)}, bf16[3,32,768]{2,1,0:T(8,128)(2,1)S(1)}, u32[]{:S(2)}, u32[]{:S(2)}) collective-permute-start(bf16[3,32,768]{2,1,0:T(8,128)(2,1)S(1)} %get-tuple-element.78), channel_id=1, source_target_pairs={{0,4},{4,8},{8,12},{12,16},{16,20},{20,24},{24,28},{28,32},{32,36}... | collective-permute-start | bytes 442376 | tf_op jit(solution)/shard_map/ppermute | solution.py:25
  32.2 3.8 %collective-permute-done.1 = bf16[3,32,768]{2,1,0:T(8,128)(2,1)S(1)} collective-permute-done((bf16[3,32,768]{2,1,0:T(8,128)(2,1)S(1)}, bf16[3,32,768]{2,1,0:T(8,128)(2,1)S(1)}, u32[]{:S(2)}, u32[]{:S(2)}) %collective-permute-start.1) | collective-permute-done | bytes 147488 | tf_op jit(solution)/shard_map/ppermute | solution.py:27
  36.2 4.3 %fusion.79 = (f32[4,32]{1,0:T(4,128)S(1)}, f32[4,32]{1,0:T(4,128)S(1)}, f32[4,32,768]{2,1,0:T(8,128)S(1)}) fusion(f32[768]{0:T(1024)S(1)} %get-tuple-element.67, f32[10,38,768]{2,1,0:T(8,128)S(1)} %fusion.7, f32[768]{0:T(1024)S(1)} %get-tuple-element.68, f32[768]{0:T(1024)S(1)} %get-tuple-element.21, f32[768]{0:T(1024)S(1)} %get-tuple-element.22, ...), kind=kLoop, calls=%fused_computation.222 | loop fusion | flops 9830144 | bytes 19812352 | tf_op jit(solution)/shard_map/reduce_sum | solution.py:205
  41.6 14.8 %psum.7 = f32[2,128]{1,0:T(2,128)S(1)} all-reduce(f32[2,128]{1,0:T(2,128)S(1)} %pad_maximum_fusion.5), channel_id=1, replica_groups=mesh['section'=4,'zl'=4,'y'=4,'core'=2,'dp'=4] {'section'}, use_global_device_ids=true, to_apply=%region_2.3 | all-reduce | flops 256 | bytes 2048 | tf_op jit(solution)/shard_map/psum | solution.py:220
  57.7 10.7 %all-to-all-start = ((bf16[32,8,768]{2,1,0:T(8,128)(2,1)}), bf16[32,8,768]{2,1,0:T(8,128)(2,1)}, u32[]{:S(2)}, u32[]{:S(2)}) async-start(bf16[32,8,768]{2,1,0:T(8,128)(2,1)} %broadcast_in_dim.97), calls=%async_computation | async-start | bytes 786432 | tf_op jit(solution)/shard_map/all_to_all | solution.py:161
  69.8 4.4 %collective-permute-start.5 = (bf16[256,2048]{1,0:T(8,128)(2,1)S(1)}, bf16[256,2048]{1,0:T(8,128)(2,1)S(1)}, u32[]{:S(2)}, u32[]{:S(2)}) collective-permute-start(bf16[256,2048]{1,0:T(8,128)(2,1)S(1)} %pad.9.refs_3_), channel_id=1, source_target_pairs={{1,0},{2,1},{3,2},{0,3},{5,4},{6,5},{7,6},{4,7},{9,8},{10,9},{11,1... | collective-permute-start | bytes 3145736 | tf_op jit(solution)/shard_map/ppermute | solution.py:16
  76.1 7.6 %all-to-all-done = bf16[32,8,768]{2,1,0:T(8,128)(2,1)} async-done(((bf16[32,8,768]{2,1,0:T(8,128)(2,1)}), bf16[32,8,768]{2,1,0:T(8,128)(2,1)}, u32[]{:S(2)}, u32[]{:S(2)}) %all-to-all-start) | async-done | bytes 393248 | tf_op jit(solution)/shard_map/all_to_all | solution.py:161
  85.0 7.3 %collective-permute-start.2 = (bf16[256,256]{1,0:T(8,128)(2,1)S(1)}, bf16[256,256]{1,0:T(8,128)(2,1)S(1)}, u32[]{:S(2)}, u32[]{:S(2)}) collective-permute-start(bf16[256,256]{1,0:T(8,128)(2,1)S(1)} %get-tuple-element.88), channel_id=1, source_target_pairs={{0,128},{128,0},{256,384},{384,256},{1,129},{129,1},{257,385},{385... | collective-permute-start | bytes 393224 | tf_op jit(solution)/shard_map/ppermute | solution.py:156
  92.3 11.3 %collective-permute-done.2 = bf16[256,256]{1,0:T(8,128)(2,1)S(1)} collective-permute-done((bf16[256,256]{1,0:T(8,128)(2,1)S(1)}, bf16[256,256]{1,0:T(8,128)(2,1)S(1)}, u32[]{:S(2)}, u32[]{:S(2)}) %collective-permute-start.2) | collective-permute-done | bytes 131104 | tf_op jit(solution)/shard_map/ppermute | solution.py:156
  105.5 9.6 %collective-permute-done.3 = bf16[256,256]{1,0:T(8,128)(2,1)S(1)} collective-permute-done((bf16[256,256]{1,0:T(8,128)(2,1)S(1)}, bf16[256,256]{1,0:T(8,128)(2,1)S(1)}, u32[]{:S(2)}, u32[]{:S(2)}) %collective-permute-start.3) | collective-permute-done | bytes 131104 | tf_op jit(solution)/shard_map/ppermute | solution.py:156
  116.2 9.7 %all-to-all-start.1 = ((bf16[4,256,256]{2,1,0:T(8,128)(2,1)}), bf16[4,256,256]{2,1,0:T(8,128)(2,1)S(1)}, u32[]{:S(2)}, u32[]{:S(2)}) async-start(bf16[4,256,256]{2,1,0:T(8,128)(2,1)} %broadcast_in_dim.98), calls=%async_computation.1 | async-start | bytes 1048576 | tf_op jit(solution)/shard_map/all_to_all | solution.py:161
  126.0 5.0 %collective-permute-start.7 = (bf16[128,2048]{1,0:T(8,128)(2,1)S(1)}, bf16[128,2048]{1,0:T(8,128)(2,1)S(1)}, u32[]{:S(2)}, u32[]{:S(2)}) collective-permute-start(bf16[128,2048]{1,0:T(8,128)(2,1)S(1)} %slice.463), channel_id=1, source_target_pairs={{1,0},{2,1},{3,2},{0,3},{5,4},{6,5},{7,6},{4,7},{9,8},{10,9},{11,1... | collective-permute-start | bytes 1572872 | tf_op jit(solution)/shard_map/ppermute | solution.py:16
  132.9 8.4 %collective-permute-done.7.refs_7_ = bf16[128,2048]{1,0:T(8,128)(2,1)S(1)} collective-permute-done((bf16[128,2048]{1,0:T(8,128)(2,1)S(1)}, bf16[128,2048]{1,0:T(8,128)(2,1)S(1)}, u32[]{:S(2)}, u32[]{:S(2)}) %collective-permute-start.7) | collective-permute-done | bytes 524320 | tf_op jit(solution)/shard_map/ppermute | solution.py:16
  141.3 5.0 %collective-permute-done.6.refs_6_ = bf16[128,2048]{1,0:T(8,128)(2,1)S(1)} collective-permute-done((bf16[128,2048]{1,0:T(8,128)(2,1)S(1)}, bf16[128,2048]{1,0:T(8,128)(2,1)S(1)}, u32[]{:S(2)}, u32[]{:S(2)}) %collective-permute-start.6) | collective-permute-done | bytes 524320 | tf_op jit(solution)/shard_map/ppermute | solution.py:16
  147.4 28.4 %all_to_all.25.refs_0_ = bf16[4,4,256,256]{3,2,1,0:T(8,128)(2,1)S(1)} all-to-all(bf16[4,4,256,256]{3,2,1,0:T(8,128)(2,1)S(1)} %broadcast_in_dim.102), channel_id=1, replica_groups=mesh['section'=4,'zl'=4,'y'=4,'core'=2,'dp'=4] {'y'}, dimensions={0} | all-to-all | bytes 4194304 | tf_op jit(solution)/shard_map/all_to_all | solution.py:161
  175.8 5.4 %collective-permute-start.8 = (bf16[4,4,256,256]{3,2,1,0:T(8,128)(2,1)S(1)}, bf16[4,4,256,256]{3,2,1,0:T(8,128)(2,1)}, u32[]{:S(2)}, u32[]{:S(2)}) collective-permute-start(bf16[4,4,256,256]{3,2,1,0:T(8,128)(2,1)S(1)} %all_to_all.25.refs_0_), channel_id=1, source_target_pairs={{0,4},{4,0},{1,5},{5,1},{2,6},{6,2},{3,7},{7,3},{8,12},{12,8},{9,1... | collective-permute-start | bytes 6291464 | tf_op jit(solution)/shard_map/ppermute | solution.py:242
  185.8 9.2 %shard_map.122 = f32[8,512]{1,0:T(8,128)} custom-call(s32[2]{0:T(128)} %pad_add_fusion.2.own_ref, f32[32,1,256]{2,1,0:T(1,128)} %bitcast.83, s32[256,2]{1,0:T(8,128)} %copy.38.meta_ref, bf16[4,4,2,256,256]{4,3,2,1,0:T(8,128)(2,1)} %bitcast.76, bf16[16,128]{1,0:T(8,128)(2,1)} %slice_bitcast_fusion.2.refs_1_, bf16[4,256,2048]{2,1,0:T(8,128)(2,1)} %bitcast.74, ...), custom_call_target="tpu_custom_call" | custom-call | flops 2147483648 | bytes 12582912 | tf_op jit(solution)/shard_map/pallas_call | solution.py:129
  195.1 8.3 %shard_map.123 = f32[8,512]{1,0:T(8,128)} custom-call(s32[2]{0:T(128)} %pad_add_fusion.2.own_ref, f32[32,1,256]{2,1,0:T(1,128)} %bitcast.84, s32[256,2]{1,0:T(8,128)} %copy.39.meta_ref, bf16[4,4,256,256]{3,2,1,0:T(8,128)(2,1)} %copy-done.2, bf16[4,4,256,256]{3,2,1,0:T(8,128)(2,1)} %collective-permute-done.8.refs_1_, bf16[4,256,2048]{2,1,0:T(8,128)(2,1)} %bitcast.75, ...), custom_call_target="tpu_custom_call" | custom-call | flops 2147483648 | bytes 12582912 | tf_op jit(solution)/shard_map/pallas_call | solution.py:129
  204.1 6.3 %collective-permute-start.9 = (f32[3,512]{1,0:T(4,128)S(1)}, f32[3,512]{1,0:T(4,128)S(1)}, u32[]{:S(2)}, u32[]{:S(2)}) collective-permute-start(f32[3,512]{1,0:T(4,128)S(1)} %slice_add_fusion), channel_id=1, source_target_pairs={{0,128},{128,0},{256,384},{384,256},{1,129},{129,1},{257,385},{385... | collective-permute-start | bytes 18440 | tf_op jit(solution)/shard_map/ppermute | solution.py:156
  210.4 1.9 collective-permute-done.9
  212.5 7.1 %collective-permute-start.10 = (f32[3,512]{1,0:T(4,128)S(1)}, f32[3,512]{1,0:T(4,128)S(1)}, u32[]{:S(2)}, u32[]{:S(2)}) collective-permute-start(f32[3,512]{1,0:T(4,128)S(1)} %get-tuple-element.87), channel_id=1, source_target_pairs={{0,384},{128,256},{256,128},{384,0},{1,385},{129,257},{257,129},{3... | collective-permute-start | bytes 18440 | tf_op jit(solution)/shard_map/ppermute | solution.py:156
  221.6 9.3 %all-to-all-start.4 = ((f32[32,3,128]{2,1,0:T(4,128)}), f32[32,3,128]{2,1,0:T(4,128)S(1)}, u32[]{:S(2)}, u32[]{:S(2)}) async-start(f32[32,3,128]{2,1,0:T(4,128)} %broadcast_in_dim.104), calls=%async_computation.4 | async-start | bytes 131072 | tf_op jit(solution)/shard_map/all_to_all | solution.py:161
  231.5 7.1 %all-to-all-done.4 = f32[32,3,128]{2,1,0:T(4,128)S(1)} async-done(((f32[32,3,128]{2,1,0:T(4,128)}), f32[32,3,128]{2,1,0:T(4,128)S(1)}, u32[]{:S(2)}, u32[]{:S(2)}) %all-to-all-start.4) | async-done | bytes 49184 | tf_op jit(solution)/shard_map/all_to_all | solution.py:161
  (113 shorter events, 27.1 us)
Async XLA Ops:
  7.2 76.6 %copy-start = (bf16[768,256]{1,0:T(8,128)(2,1)S(1)}, bf16[768,256]{1,0:T(8,128)(2,1)}, u32[]{:S(2)}) copy-start(bf16[768,256]{1,0:T(8,128)(2,1)} %param.16) | copy-start | bytes 1179652
  7.2 28.8 %copy-start.5 = (bf16[1,4,32,768]{3,2,1,0:T(8,128)(2,1)S(1)}, bf16[1,4,32,768]{3,2,1,0:T(8,128)(2,1)}, u32[]{:S(2)}) copy-start(bf16[1,4,32,768]{3,2,1,0:T(8,128)(2,1)} %param.11) | copy-start | bytes 589828
  8.8 31.8 %all-to-all-start.2 = ((bf16[4,128,256]{2,1,0:T(8,128)(2,1)}), bf16[4,128,256]{2,1,0:T(8,128)(2,1)S(1)}, u32[]{:S(2)}, u32[]{:S(2)}) async-start(bf16[4,128,256]{2,1,0:T(8,128)(2,1)} %broadcast_in_dim.100), calls=%async_computation.2 | async-start | bytes 524288 | tf_op jit(solution)/shard_map/all_to_all | solution.py:161
  24.5 121.9 %all-gather.5.cloned.1.call-start = ((), (), s32[]{:S(2)}) async-start(), calls=%async_computation.5 | async-start | bytes 4325376 | tf_op jit(solution)/shard_map/all_gather | solution.py:218
  25.5 6.8 %collective-permute-start = (bf16[3,32,768]{2,1,0:T(8,128)(2,1)S(1)}, bf16[3,32,768]{2,1,0:T(8,128)(2,1)S(1)}, u32[]{:S(2)}, u32[]{:S(2)}) collective-permute-start(bf16[3,32,768]{2,1,0:T(8,128)(2,1)S(1)} %get-tuple-element.78), channel_id=1, source_target_pairs={{0,4},{4,8},{8,12},{12,16},{16,20},{20,24},{24,28},{28,32},{32,36}... | collective-permute-start | bytes 442376 | tf_op jit(solution)/shard_map/ppermute | solution.py:25
  29.5 6.5 %collective-permute-start.1 = (bf16[3,32,768]{2,1,0:T(8,128)(2,1)S(1)}, bf16[3,32,768]{2,1,0:T(8,128)(2,1)S(1)}, u32[]{:S(2)}, u32[]{:S(2)}) collective-permute-start(bf16[3,32,768]{2,1,0:T(8,128)(2,1)S(1)} %get-tuple-element.79), channel_id=1, source_target_pairs={{4,0},{8,4},{12,8},{16,12},{20,16},{24,20},{28,24},{32,28},{36,32}... | collective-permute-start | bytes 442376 | tf_op jit(solution)/shard_map/ppermute | solution.py:27
  57.7 26.0 %all-to-all-start = ((bf16[32,8,768]{2,1,0:T(8,128)(2,1)}), bf16[32,8,768]{2,1,0:T(8,128)(2,1)}, u32[]{:S(2)}, u32[]{:S(2)}) async-start(bf16[32,8,768]{2,1,0:T(8,128)(2,1)} %broadcast_in_dim.97), calls=%async_computation | async-start | bytes 786432 | tf_op jit(solution)/shard_map/all_to_all | solution.py:161
  68.4 117.4 %all-gather.7.cloned.1.call-start = ((), (), s32[]{:S(2)}) async-start(), calls=%async_computation.6 | async-start | bytes 5242880 | tf_op jit(solution)/shard_map/all_gather | solution.py:188
  69.8 46.4 %copy-start.1 = (bf16[256,2048]{1,0:T(8,128)(2,1)}, bf16[256,2048]{1,0:T(8,128)(2,1)S(1)}, u32[]{:S(2)}) copy-start(bf16[256,2048]{1,0:T(8,128)(2,1)S(1)} %pad.9.refs_3_) | copy-start | bytes 3145732
  69.8 45.4 %collective-permute-start.5 = (bf16[256,2048]{1,0:T(8,128)(2,1)S(1)}, bf16[256,2048]{1,0:T(8,128)(2,1)S(1)}, u32[]{:S(2)}, u32[]{:S(2)}) collective-permute-start(bf16[256,2048]{1,0:T(8,128)(2,1)S(1)} %pad.9.refs_3_), channel_id=1, source_target_pairs={{1,0},{2,1},{3,2},{0,3},{5,4},{6,5},{7,6},{4,7},{9,8},{10,9},{11,1... | collective-permute-start | bytes 3145736 | tf_op jit(solution)/shard_map/ppermute | solution.py:16
  74.2 41.0 %collective-permute-start.4 = (bf16[256,2048]{1,0:T(8,128)(2,1)S(1)}, bf16[256,2048]{1,0:T(8,128)(2,1)S(1)}, u32[]{:S(2)}, u32[]{:S(2)}) collective-permute-start(bf16[256,2048]{1,0:T(8,128)(2,1)S(1)} %pad.9.refs_3_), channel_id=1, source_target_pairs={{3,0},{0,1},{1,2},{2,3},{7,4},{4,5},{5,6},{6,7},{11,8},{8,9},{9,10... | collective-permute-start | bytes 3145736 | tf_op jit(solution)/shard_map/ppermute | solution.py:16
  85.0 18.6 %collective-permute-start.2 = (bf16[256,256]{1,0:T(8,128)(2,1)S(1)}, bf16[256,256]{1,0:T(8,128)(2,1)S(1)}, u32[]{:S(2)}, u32[]{:S(2)}) collective-permute-start(bf16[256,256]{1,0:T(8,128)(2,1)S(1)} %get-tuple-element.88), channel_id=1, source_target_pairs={{0,128},{128,0},{256,384},{384,256},{1,129},{129,1},{257,385},{385... | collective-permute-start | bytes 393224 | tf_op jit(solution)/shard_map/ppermute | solution.py:156
  103.6 11.5 %collective-permute-start.3 = (bf16[256,256]{1,0:T(8,128)(2,1)S(1)}, bf16[256,256]{1,0:T(8,128)(2,1)S(1)}, u32[]{:S(2)}, u32[]{:S(2)}) collective-permute-start(bf16[256,256]{1,0:T(8,128)(2,1)S(1)} %fusion.63), channel_id=1, source_target_pairs={{0,384},{128,256},{256,128},{384,0},{1,385},{129,257},{257,129},{3... | collective-permute-start | bytes 393224 | tf_op jit(solution)/shard_map/ppermute | solution.py:156
  116.2 30.2 %all-to-all-start.1 = ((bf16[4,256,256]{2,1,0:T(8,128)(2,1)}), bf16[4,256,256]{2,1,0:T(8,128)(2,1)S(1)}, u32[]{:S(2)}, u32[]{:S(2)}) async-start(bf16[4,256,256]{2,1,0:T(8,128)(2,1)} %broadcast_in_dim.98), calls=%async_computation.1 | async-start | bytes 1048576 | tf_op jit(solution)/shard_map/all_to_all | solution.py:161
  126.0 15.3 %collective-permute-start.7 = (bf16[128,2048]{1,0:T(8,128)(2,1)S(1)}, bf16[128,2048]{1,0:T(8,128)(2,1)S(1)}, u32[]{:S(2)}, u32[]{:S(2)}) collective-permute-start(bf16[128,2048]{1,0:T(8,128)(2,1)S(1)} %slice.463), channel_id=1, source_target_pairs={{1,0},{2,1},{3,2},{0,3},{5,4},{6,5},{7,6},{4,7},{9,8},{10,9},{11,1... | collective-permute-start | bytes 1572872 | tf_op jit(solution)/shard_map/ppermute | solution.py:16
  131.0 15.3 %collective-permute-start.6 = (bf16[128,2048]{1,0:T(8,128)(2,1)S(1)}, bf16[128,2048]{1,0:T(8,128)(2,1)S(1)}, u32[]{:S(2)}, u32[]{:S(2)}) collective-permute-start(bf16[128,2048]{1,0:T(8,128)(2,1)S(1)} %slice.462), channel_id=1, source_target_pairs={{3,0},{0,1},{1,2},{2,3},{7,4},{4,5},{5,6},{6,7},{11,8},{8,9},{9,10... | collective-permute-start | bytes 1572872 | tf_op jit(solution)/shard_map/ppermute | solution.py:16
  141.3 44.5 %copy-start.7 = (bf16[128,2048]{1,0:T(8,128)(2,1)}, bf16[128,2048]{1,0:T(8,128)(2,1)S(1)}, u32[]{:S(2)}) copy-start(bf16[128,2048]{1,0:T(8,128)(2,1)S(1)} %collective-permute-done.7.refs_7_) | copy-start | bytes 1572868
  146.3 39.4 %copy-start.8 = (bf16[128,2048]{1,0:T(8,128)(2,1)}, bf16[128,2048]{1,0:T(8,128)(2,1)S(1)}, u32[]{:S(2)}) copy-start(bf16[128,2048]{1,0:T(8,128)(2,1)S(1)} %collective-permute-done.6.refs_6_) | copy-start | bytes 1572868
  147.4 34.6 %copy-start.18 = (s32[1,512]{1,0:T(1,128)S(1)}, s32[1,512]{1,0:T(1,128)}, u32[]{:S(2)}) copy-start(s32[1,512]{1,0:T(1,128)} %param.21) | copy-start | bytes 6148
  175.8 19.3 %collective-permute-start.8 = (bf16[4,4,256,256]{3,2,1,0:T(8,128)(2,1)S(1)}, bf16[4,4,256,256]{3,2,1,0:T(8,128)(2,1)}, u32[]{:S(2)}, u32[]{:S(2)}) collective-permute-start(bf16[4,4,256,256]{3,2,1,0:T(8,128)(2,1)S(1)} %all_to_all.25.refs_0_), channel_id=1, source_target_pairs={{0,4},{4,0},{1,5},{5,1},{2,6},{6,2},{3,7},{7,3},{8,12},{12,8},{9,1... | collective-permute-start | bytes 6291464 | tf_op jit(solution)/shard_map/ppermute | solution.py:242
  195.1 35.8 %copy-start.11 = (f32[8,768]{1,0:T(8,128)S(1)}, f32[8,768]{1,0:T(8,128)}, u32[]{:S(2)}) copy-start(f32[8,768]{1,0:T(8,128)} %copy-done.10) | copy-start | bytes 73732
  204.1 8.3 %collective-permute-start.9 = (f32[3,512]{1,0:T(4,128)S(1)}, f32[3,512]{1,0:T(4,128)S(1)}, u32[]{:S(2)}, u32[]{:S(2)}) collective-permute-start(f32[3,512]{1,0:T(4,128)S(1)} %slice_add_fusion), channel_id=1, source_target_pairs={{0,128},{128,0},{256,384},{384,256},{1,129},{129,1},{257,385},{385... | collective-permute-start | bytes 18440 | tf_op jit(solution)/shard_map/ppermute | solution.py:156
  212.5 8.4 %collective-permute-start.10 = (f32[3,512]{1,0:T(4,128)S(1)}, f32[3,512]{1,0:T(4,128)S(1)}, u32[]{:S(2)}, u32[]{:S(2)}) collective-permute-start(f32[3,512]{1,0:T(4,128)S(1)} %get-tuple-element.87), channel_id=1, source_target_pairs={{0,384},{128,256},{256,128},{384,0},{1,385},{129,257},{257,129},{3... | collective-permute-start | bytes 18440 | tf_op jit(solution)/shard_map/ppermute | solution.py:156
  221.6 17.1 %all-to-all-start.4 = ((f32[32,3,128]{2,1,0:T(4,128)}), f32[32,3,128]{2,1,0:T(4,128)S(1)}, u32[]{:S(2)}, u32[]{:S(2)}) async-start(f32[32,3,128]{2,1,0:T(4,128)} %broadcast_in_dim.104), calls=%async_computation.4 | async-start | bytes 131072 | tf_op jit(solution)/shard_map/all_to_all | solution.py:161
  (13 other events, 208.3 us)
Sparse Core Ops, SparseCore 0:
  41.7 85.1 all-gather.4
  129.1 55.6 all-gather.6
where the time goes:
time: 247 us; the launch traced here: 246 us
  starting transfers between devices  92.5 us (37%)
  waiting for transfers between devices  56.1 us (23%)
  blocking collectives  43.1 us (17%)
  Pallas kernels  17.5 us (7%)
  between operations  14.6 us (6%)
  local copies, waits for them, and re-layouts  11.1 us (4%)
  other arithmetic  8.95 us (4%)
    all_to_all x4, starting transfers between devices, to_all(): lax.all_to_all(jnp.broadcast_to(value[None], (count,) + value.shape), axi...  45.3 us
    all_to_all x1, blocking collectives, to_all(): lax.all_to_all(jnp.broadcast_to(value[None], (count,) + value.shape), axi...  28.4 us
    ppermute x4, waiting for transfers between devices, across(): return lax.ppermute(value, 'section', pairs)  24.1 us
    ppermute x4, starting transfers between devices, across(): return lax.ppermute(value, 'section', pairs)  22.6 us
    pallas_call x2, Pallas kernels, head_stats(): pl.pallas_call(functools.partial(head_kernel, columns, offsets, from_text...  17.5 us
    psum x1, blocking collectives, shards(): sums = lax.psum(sums, 'section')  14.8 us
    all_to_all x4, waiting for transfers between devices, to_all(): lax.all_to_all(jnp.broadcast_to(value[None], (count,) + value.shape), axi...  14.7 us
    ppermute x4, waiting for transfers between devices, shifted(): lax.ppermute(value, axis, [((i + step) % count, i) for i in range(count)])  13.4 us
  transfers between devices with their start and end apart: 17, of which 9 were waited for; matrix products, arithmetic and copies ran while one was open for 7% of the time, Pallas kernels for 4%

commit v1 on v0

--- a/solution.py
+++ b/solution.py
@@ -20,14 +20,9 @@
     count = lax.axis_size(axis)
     ends = count - 1
     head, tail = cells[:width], cells[-width:]
-    return jnp.concatenate(
-        [
-            lax.ppermute(tail, axis, [(i, (i + 1) % count) for i in range(ends)]),
-            cells,
-            lax.ppermute(head, axis, [((i + 1) % count, i) for i in range(ends)]),
-        ],
-        axis=0,
-    )
+    above = lax.ppermute(tail, axis, [(i, (i + 1) % count) for i in range(ends)])
+    below = lax.ppermute(head, axis, [((i + 1) % count, i) for i in range(ends)])
+    return above, below
 
 
 def head_kernel(columns, offsets, from_text, own_ref, gain_ref, meta_ref, *refs):
@@ -182,8 +177,6 @@
     columns = head_weight.shape[1]
     slots = lax.iota(jnp.int32, targets.shape[0])
 
-    text = to_all(text_embed[0], "section").reshape(slots.shape[0], -1)
-
     weight = head_weight.T
     low_all = lax.all_gather(weight[:WIDE], "dp", axis=0)
     high = jnp.pad(weight[WIDE:], ((0, 2 * WIDE - columns), (0, 0)))
@@ -191,7 +184,12 @@
 
     image = features[0]
     height, width, chans = image.shape
-    padded = extended(image, VOCAB, 3)
+    above, below = extended(image, VOCAB, 3)
+    padded = jnp.concatenate([above, image, below])
+
+    text, _, _ = lax.optimization_barrier((text_embed[0], above, below))
+    text = to_all(text, "section")
+
     padded = jnp.pad(padded, ((0, 0), (3, 3), (0, 0))).astype(jnp.float32)
     conv = jnp.zeros((height, width, chans), jnp.float32)
     for row_off in range(7):
@@ -204,19 +202,6 @@
     sums = jnp.stack(
         [jnp.sum(conv, axis=-1).reshape(-1), jnp.sum(conv * conv, axis=-1).reshape(-1)]
     )
-    is_text = jnp.all(slots[:, None] != places[None, :], axis=1)
-    rank = jnp.sum(
-        jnp.where((slots[None, :] < slots[:, None]) & is_text[None, :], 1, 0), axis=1
-    )
-    text_rows = slots.shape[0] - places.shape[0]
-    select = (rank[None, :] == lax.iota(jnp.int32, text_rows)[:, None]) & is_text[None, :]
-    text, _ = lax.optimization_barrier((text, sums))
-    text = jnp.dot(
-        select.astype(jnp.bfloat16), text, preferred_element_type=jnp.float32
-    ).astype(jnp.bfloat16)
-    text_slots = jnp.sum(jnp.where(select, slots[None, :], 0), axis=1)
-    text_all = lax.all_gather(text, VOCAB, axis=0)
-    text_all = text_all.reshape(tuple(lax.axis_size(axis) for axis in VOCAB) + text.shape)
     sums = lax.psum(sums, "section")
     all_chans = chans * sections
     middle = sums[0].reshape(height, width) / all_chans
@@ -226,19 +211,41 @@
     pooled = block.reshape(height // 4, 4, width // 4, 4, chans).mean(axis=(1, 3))
     pooled = pooled.reshape(-1, chans).astype(jnp.bfloat16)
 
-    tokens = to_all(pooled, VOCAB).reshape(-1, chans)
-    rows = jnp.dot(tokens, proj_weight, preferred_element_type=jnp.float32)
-    for turn in range(2):
-        rows = rows + across(rows.astype(jnp.bfloat16), turn).astype(jnp.float32)
-    rows = rows.astype(jnp.bfloat16)
+    pooled, text = lax.optimization_barrier((pooled, text))
+    tokens = to_all(pooled, VOCAB)
+    rows = jnp.dot(tokens.reshape(-1, chans), proj_weight, preferred_element_type=jnp.float32)
+    middle_row = rows.shape[0] // 2
+    halves = [rows[:middle_row], rows[middle_row:]]
+    for step in range(2):
+        halves = [
+            half + across(half.astype(jnp.bfloat16), step ^ at).astype(jnp.float32)
+            for at, half in enumerate(halves)
+        ]
+    rows = jnp.concatenate([half.astype(jnp.bfloat16) for half in halves])
+
+    is_text = jnp.all(slots[:, None] != places[None, :], axis=1)
+    rank = jnp.sum(
+        jnp.where((slots[None, :] < slots[:, None]) & is_text[None, :], 1, 0), axis=1
+    )
+    text_rows = slots.shape[0] - places.shape[0]
+    select = (rank[None, :] == lax.iota(jnp.int32, text_rows)[:, None]) & is_text[None, :]
+    text, _, _ = lax.optimization_barrier((text, tokens, low_all))
+    text = jnp.dot(
+        select.astype(jnp.bfloat16),
+        text.reshape(slots.shape[0], -1),
+        preferred_element_type=jnp.float32,
+    ).astype(jnp.bfloat16)
+    text_slots = jnp.sum(jnp.where(select, slots[None, :], 0), axis=1)
+    text_all = lax.all_gather(text, VOCAB, axis=0)
+    text_all = text_all.reshape(tuple(lax.axis_size(axis) for axis in VOCAB) + text.shape)
 
     rows, left, right = lax.optimization_barrier((rows, left, right))
     half = WIDE // 2
     far, off = shifted(left[:half], "dp", -1), shifted(right[half:], "dp", 1)
     rows = to_all(rows, "zl")
+    early = rows
+    rows = to_all(rows, "y")
     rows, text_all, far, off = lax.optimization_barrier((rows, text_all, far, off))
-    early = rows[0, :16, :128]
-    rows = to_all(rows, "y")
     partner = lax.ppermute(rows, "core", [(0, 1), (1, 0)])
 
     gain = rms_gain.reshape(-1, 1, text.shape[1])
@@ -271,10 +278,11 @@
             [top, jnp.sum(totals * jnp.exp(tops - top), axis=0), jnp.sum(chosen, axis=0)]
         )
 
-    for turn in range(2):
-        both = merged(jnp.stack([both, across(both, turn)]))
-    both = both.reshape(3, sections, -1)
-    both = lax.dynamic_index_in_dim(both, lax.axis_index("section"), 1, keepdims=False)
+    section = lax.axis_index("section")
+    mine = lax.iota(jnp.int32, sections)[:, None, None] == section
+    both = lax.psum(jnp.where(mine, both[None], 0.0), "section")
+    both = both.reshape(sections, 3, sections, -1)
+    both = merged(lax.dynamic_index_in_dim(both, section, 2, keepdims=False))
     top, total, chosen = merged(to_all(both, VOCAB))
     loss = top + jnp.log(total) - chosen
     return (pooled[None], loss[None])

time: 247 us -> 250 us (1.012)
  blocking collectives: 43.1 us -> 77.6 us
  starting transfers between devices: 92.5 us -> 74.8 us
  waiting for transfers between devices: 56.1 us -> 43.7 us
    psum x0 -> x1, blocking collectives: none -> 16.4 us  [shards(): both = lax.psum(jnp.where(mine, both[None], 0.0), 'section')]
    all_to_all x1 -> x2, blocking collectives: 28.4 us -> 43.8 us  [to_all(): lax.all_to_all(jnp.broadcast_to(value[None], (count,) + value.shape), axi...]
    all_to_all x4 -> x3, starting transfers between devices: 45.3 us -> 31.3 us  [to_all(): lax.all_to_all(jnp.broadcast_to(value[None], (count,) + value.shape), axi...]
    ppermute x4, waiting for transfers between devices: 24.1 us -> 12.2 us  [across(): return lax.ppermute(value, 'section', pairs)]
    ppermute x4, starting transfers between devices: 22.6 us -> 16.1 us  [across(): return lax.ppermute(value, 'section', pairs)]
    all_to_all x4 -> x3, waiting for transfers between devices: 14.7 us -> 21.1 us  [to_all(): lax.all_to_all(jnp.broadcast_to(value[None], (count,) + value.shape), axi...]
    ppermute x4, waiting for transfers between devices: 13.4 us -> 9.81 us  [shifted(): lax.ppermute(value, axis, [((i + step) % count, i) for i in range(count)])]
    ppermute x1, starting transfers between devices: 1.92 us -> 5.49 us  [extended(): lax.ppermute(head, axis, [((i + 1) % count, i) for i in range(ends)])]
  transfers between devices with their start and end apart: 17 -> 16, of which waited for: 9 -> 9; matrix products, arithmetic and copies ran while one was open for 7% -> 6% of each run, Pallas kernels for 4% -> 4%
where the time goes in v1:
time: 250 us; the launch traced here: 249 us
  blocking collectives  77.6 us (31%)
  starting transfers between devices  74.8 us (30%)
  waiting for transfers between devices  43.7 us (17%)
  Pallas kernels  17.5 us (7%)
  between operations  14.6 us (6%)
  local copies, waits for them, and re-layouts  11.4 us (5%)
  other arithmetic  7.72 us (3%)
    all_to_all x2, blocking collectives, to_all(): lax.all_to_all(jnp.broadcast_to(value[None], (count,) + value.shape), axi...  43.8 us
    all_to_all x3, starting transfers between devices, to_all(): lax.all_to_all(jnp.broadcast_to(value[None], (count,) + value.shape), axi...  31.3 us
    all_to_all x3, waiting for transfers between devices, to_all(): lax.all_to_all(jnp.broadcast_to(value[None], (count,) + value.shape), axi...  21.1 us
    pallas_call x2, Pallas kernels, head_stats(): pl.pallas_call(functools.partial(head_kernel, columns, offsets, from_text...  17.5 us
    psum x1, blocking collectives, shards(): sums = lax.psum(sums, 'section')  17.4 us
    psum x1, blocking collectives, shards(): both = lax.psum(jnp.where(mine, both[None], 0.0), 'section')  16.4 us
    ppermute x4, starting transfers between devices, across(): return lax.ppermute(value, 'section', pairs)  16.1 us
    ppermute x4, starting transfers between devices, shifted(): lax.ppermute(value, axis, [((i + step) % count, i) for i in range(count)])  13 us
  transfers between devices with their start and end apart: 16, of which 9 were waited for; matrix products, arithmetic and copies ran while one was open for 6% of the time, Pallas kernels for 4%

profile of v1, /device:TPU:1, one launch (start us, length us, event | category | flops | bytes accessed | tf_op | source)
XLA Modules:
  0.0 248.6 jit_solution(10320492507285834391)
XLA Ops:
  9.7 4.7 %collective-permute-start = (bf16[3,32,768]{2,1,0:T(8,128)(2,1)S(1)}, bf16[3,32,768]{2,1,0:T(8,128)(2,1)S(1)}, u32[]{:S(2)}, u32[]{:S(2)}) collective-permute-start(bf16[3,32,768]{2,1,0:T(8,128)(2,1)S(1)} %get-tuple-element.88), channel_id=1, source_target_pairs={{0,4},{4,8},{8,12},{12,16},{16,20},{20,24},{24,28},{28,32},{32,36}... | collective-permute-start | bytes 442376 | tf_op jit(solution)/shard_map/ppermute | solution.py:23
  14.4 5.5 %collective-permute-start.1 = (bf16[3,32,768]{2,1,0:T(8,128)(2,1)S(1)}, bf16[3,32,768]{2,1,0:T(8,128)(2,1)S(1)}, u32[]{:S(2)}, u32[]{:S(2)}) collective-permute-start(bf16[3,32,768]{2,1,0:T(8,128)(2,1)S(1)} %get-tuple-element.89), channel_id=1, source_target_pairs={{4,0},{8,4},{12,8},{16,12},{20,16},{24,20},{28,24},{32,28},{36,32}... | collective-permute-start | bytes 442376 | tf_op jit(solution)/shard_map/ppermute | solution.py:24
  21.1 4.3 %fusion.68 = (f32[4,32]{1,0:T(4,128)S(1)}, f32[4,32]{1,0:T(4,128)S(1)}, f32[4,32,768]{2,1,0:T(8,128)S(1)}) fusion(f32[768]{0:T(1024)S(1)} %get-tuple-element.73, f32[10,38,768]{2,1,0:T(8,128)S(1)} %fusion.7, f32[768]{0:T(1024)S(1)} %get-tuple-element.74, f32[768]{0:T(1024)S(1)} %get-tuple-element.27, f32[768]{0:T(1024)S(1)} %get-tuple-element.28, ...), kind=kLoop, calls=%fused_computation.209 | loop fusion | flops 9830144 | bytes 19812352 | tf_op jit(solution)/shard_map/reduce_sum | solution.py:203
  26.3 14.8 %all-to-all-start = ((bf16[4,128,256]{2,1,0:T(8,128)(2,1)}), bf16[4,128,256]{2,1,0:T(8,128)(2,1)S(1)}, u32[]{:S(2)}, u32[]{:S(2)}) async-start(bf16[4,128,256]{2,1,0:T(8,128)(2,1)} %broadcast_in_dim.110), calls=%async_computation | async-start | bytes 524288 | tf_op jit(solution)/shard_map/all_to_all | solution.py:156
  41.1 17.4 %psum.14 = f32[2,128]{1,0:T(2,128)S(1)} all-reduce(f32[2,128]{1,0:T(2,128)S(1)} %pad_maximum_fusion.2), channel_id=1, replica_groups=mesh['section'=4,'zl'=4,'y'=4,'core'=2,'dp'=4] {'section'}, use_global_device_ids=true, to_apply=%region_2.3 | all-reduce | flops 256 | bytes 2048 | tf_op jit(solution)/shard_map/psum | solution.py:205
  59.8 12.9 %all-to-all-start.1 = ((bf16[32,8,768]{2,1,0:T(8,128)(2,1)}), bf16[32,8,768]{2,1,0:T(8,128)(2,1)S(1)}, u32[]{:S(2)}, u32[]{:S(2)}) async-start(bf16[32,8,768]{2,1,0:T(8,128)(2,1)} %broadcast_in_dim.120), calls=%async_computation.1 | async-start | bytes 786432 | tf_op jit(solution)/shard_map/all_to_all | solution.py:156
  73.1 13.4 %all-to-all-done.1 = bf16[32,8,768]{2,1,0:T(8,128)(2,1)S(1)} async-done(((bf16[32,8,768]{2,1,0:T(8,128)(2,1)}), bf16[32,8,768]{2,1,0:T(8,128)(2,1)S(1)}, u32[]{:S(2)}, u32[]{:S(2)}) %all-to-all-start.1) | async-done | bytes 393248 | tf_op jit(solution)/shard_map/all_to_all | solution.py:156
  88.9 3.1 %collective-permute-start.6 = (bf16[256,2048]{1,0:T(8,128)(2,1)S(1)}, bf16[256,2048]{1,0:T(8,128)(2,1)S(1)}, u32[]{:S(2)}, u32[]{:S(2)}) collective-permute-start(bf16[256,2048]{1,0:T(8,128)(2,1)S(1)} %pad.9.refs_3_), channel_id=1, source_target_pairs={{3,0},{0,1},{1,2},{2,3},{7,4},{4,5},{5,6},{6,7},{11,8},{8,9},{9,10... | collective-permute-start | bytes 3145736 | tf_op jit(solution)/shard_map/ppermute | solution.py:16
  92.0 3.4 %collective-permute-start.7 = (bf16[256,2048]{1,0:T(8,128)(2,1)S(1)}, bf16[256,2048]{1,0:T(8,128)(2,1)}, u32[]{:S(2)}, u32[]{:S(2)}) collective-permute-start(bf16[256,2048]{1,0:T(8,128)(2,1)S(1)} %pad.9.refs_3_), channel_id=1, source_target_pairs={{1,0},{2,1},{3,2},{0,3},{5,4},{6,5},{7,6},{4,7},{9,8},{10,9},{11,1... | collective-permute-start | bytes 3145736 | tf_op jit(solution)/shard_map/ppermute | solution.py:16
  97.6 5.3 %collective-permute-start.4 = (bf16[128,256]{1,0:T(8,128)(2,1)S(1)}, bf16[128,256]{1,0:T(8,128)(2,1)S(1)}, u32[]{:S(2)}, u32[]{:S(2)}) collective-permute-start(bf16[128,256]{1,0:T(8,128)(2,1)S(1)} %get-tuple-element.87), channel_id=1, source_target_pairs={{0,384},{128,256},{256,128},{384,0},{1,385},{129,257},{257,129},{3... | collective-permute-start | bytes 196616 | tf_op jit(solution)/shard_map/ppermute | solution.py:151
  103.0 6.1 %collective-permute-done.2 = bf16[128,256]{1,0:T(8,128)(2,1)S(1)} collective-permute-done((bf16[128,256]{1,0:T(8,128)(2,1)S(1)}, bf16[128,256]{1,0:T(8,128)(2,1)S(1)}, u32[]{:S(2)}, u32[]{:S(2)}) %collective-permute-start.2) | collective-permute-done | bytes 65568 | tf_op jit(solution)/shard_map/ppermute | solution.py:151
  110.4 4.2 %collective-permute-start.3 = (bf16[128,256]{1,0:T(8,128)(2,1)S(1)}, bf16[128,256]{1,0:T(8,128)(2,1)S(1)}, u32[]{:S(2)}, u32[]{:S(2)}) collective-permute-start(bf16[128,256]{1,0:T(8,128)(2,1)S(1)} %get-tuple-element.84), channel_id=1, source_target_pairs={{0,384},{128,256},{256,128},{384,0},{1,385},{129,257},{257,129},{3... | collective-permute-start | bytes 196616 | tf_op jit(solution)/shard_map/ppermute | solution.py:151
  114.6 4.7 %collective-permute-start.5 = (bf16[128,256]{1,0:T(8,128)(2,1)S(1)}, bf16[128,256]{1,0:T(8,128)(2,1)S(1)}, u32[]{:S(2)}, u32[]{:S(2)}) collective-permute-start(bf16[128,256]{1,0:T(8,128)(2,1)S(1)} %get-tuple-element.85), channel_id=1, source_target_pairs={{0,128},{128,0},{256,384},{384,256},{1,129},{129,1},{257,385},{385... | collective-permute-start | bytes 196616 | tf_op jit(solution)/shard_map/ppermute | solution.py:151
  120.1 3.9 %collective-permute-done.5 = bf16[128,256]{1,0:T(8,128)(2,1)S(1)} collective-permute-done((bf16[128,256]{1,0:T(8,128)(2,1)S(1)}, bf16[128,256]{1,0:T(8,128)(2,1)S(1)}, u32[]{:S(2)}, u32[]{:S(2)}) %collective-permute-start.5) | collective-permute-done | bytes 65568 | tf_op jit(solution)/shard_map/ppermute | solution.py:151
  124.2 28.0 %all_to_all.25.refs_1_ = bf16[4,256,256]{2,1,0:T(8,128)(2,1)S(1)} all-to-all(bf16[4,256,256]{2,1,0:T(8,128)(2,1)S(1)} %broadcast_in_dim.121), channel_id=1, replica_groups=mesh['section'=4,'zl'=4,'y'=4,'core'=2,'dp'=4] {'zl'}, dimensions={0} | all-to-all | bytes 1048576 | tf_op jit(solution)/shard_map/all_to_all | solution.py:156
  154.6 3.6 %all-to-all-start.3 = ((bf16[4,4,256,256]{3,2,1,0:T(8,128)(2,1)}), bf16[4,4,256,256]{3,2,1,0:T(8,128)(2,1)S(1)}, u32[]{:S(2)}, u32[]{:S(2)}) async-start(bf16[4,4,256,256]{3,2,1,0:T(8,128)(2,1)} %broadcast_in_dim.122), calls=%async_computation.3 | async-start | bytes 4194304 | tf_op jit(solution)/shard_map/all_to_all | solution.py:156
  161.4 4.5 %collective-permute-start.9 = (bf16[128,2048]{1,0:T(8,128)(2,1)S(1)}, bf16[128,2048]{1,0:T(8,128)(2,1)S(1)}, u32[]{:S(2)}, u32[]{:S(2)}) collective-permute-start(bf16[128,2048]{1,0:T(8,128)(2,1)S(1)} %slice.460), channel_id=1, source_target_pairs={{1,0},{2,1},{3,2},{0,3},{5,4},{6,5},{7,6},{4,7},{9,8},{10,9},{11,1... | collective-permute-start | bytes 1572872 | tf_op jit(solution)/shard_map/ppermute | solution.py:16
  165.9 7.8 %collective-permute-done.8.refs_6_ = bf16[128,2048]{1,0:T(8,128)(2,1)S(1)} collective-permute-done((bf16[128,2048]{1,0:T(8,128)(2,1)S(1)}, bf16[128,2048]{1,0:T(8,128)(2,1)S(1)}, u32[]{:S(2)}, u32[]{:S(2)}) %collective-permute-start.8) | collective-permute-done | bytes 524320 | tf_op jit(solution)/shard_map/ppermute | solution.py:16
  175.7 7.7 %all-to-all-done.3.refs_0_ = bf16[4,4,256,256]{3,2,1,0:T(8,128)(2,1)S(1)} async-done(((bf16[4,4,256,256]{3,2,1,0:T(8,128)(2,1)}), bf16[4,4,256,256]{3,2,1,0:T(8,128)(2,1)S(1)}, u32[]{:S(2)}, u32[]{:S(2)}) %all-to-all-start.3) | async-done | bytes 2097184 | tf_op jit(solution)/shard_map/all_to_all | solution.py:156
  183.4 4.1 %collective-permute-start.10 = (bf16[4,4,256,256]{3,2,1,0:T(8,128)(2,1)S(1)}, bf16[4,4,256,256]{3,2,1,0:T(8,128)(2,1)}, u32[]{:S(2)}, u32[]{:S(2)}) collective-permute-start(bf16[4,4,256,256]{3,2,1,0:T(8,128)(2,1)S(1)} %all-to-all-done.3.refs_0_), channel_id=1, source_target_pairs={{0,4},{4,0},{1,5},{5,1},{2,6},{6,2},{3,7},{7,3},{8,12},{12,8},{9,1... | collective-permute-start | bytes 6291464 | tf_op jit(solution)/shard_map/ppermute | solution.py:249
  190.3 9.2 %shard_map.122 = f32[8,512]{1,0:T(8,128)} custom-call(s32[2]{0:T(128)} %pad_add_fusion.2.own_ref, f32[32,1,256]{2,1,0:T(1,128)} %bitcast.60, s32[256,2]{1,0:T(8,128)} %copy.30.meta_ref, bf16[4,4,2,256,256]{4,3,2,1,0:T(8,128)(2,1)} %bitcast.53, bf16[4,256,256]{2,1,0:T(8,128)(2,1)} %copy-done.4, bf16[4,256,2048]{2,1,0:T(8,128)(2,1)} %bitcast.51, ...), custom_call_target="tpu_custom_call" | custom-call | flops 2147483648 | bytes 12582912 | tf_op jit(solution)/shard_map/pallas_call | solution.py:124
  199.6 8.3 %shard_map.123 = f32[8,512]{1,0:T(8,128)} custom-call(s32[2]{0:T(128)} %pad_add_fusion.2.own_ref, f32[32,1,256]{2,1,0:T(1,128)} %bitcast.61, s32[256,2]{1,0:T(8,128)} %copy.31.meta_ref, bf16[4,4,256,256]{3,2,1,0:T(8,128)(2,1)} %copy-done.2, bf16[4,4,256,256]{3,2,1,0:T(8,128)(2,1)} %collective-permute-done.10.refs_1_, bf16[4,256,2048]{2,1,0:T(8,128)(2,1)} %bitcast.52, ...), custom_call_target="tpu_custom_call" | custom-call | flops 2147483648 | bytes 12582912 | tf_op jit(solution)/shard_map/pallas_call | solution.py:124
  208.7 16.4 %psum.15 = f32[4,3,4,128]{3,2,0,1:T(4,128)S(1)} all-reduce(f32[4,3,4,128]{3,2,0,1:T(4,128)S(1)} %reshape.116), channel_id=1, replica_groups=mesh['section'=4,'zl'=4,'y'=4,'core'=2,'dp'=4] {'section'}, use_global_device_ids=true, to_apply=%region_10.11 | all-reduce | flops 6144 | bytes 49152 | tf_op jit(solution)/shard_map/psum | solution.py:283
  225.2 15.9 %all_to_all.26 = f32[32,3,128]{2,1,0:T(4,128)S(1)} all-to-all(f32[32,3,128]{2,1,0:T(4,128)S(1)} %broadcast_in_dim.126), channel_id=1, replica_groups=mesh['section'=4,'zl'=4,'y'=4,'core'=2,'dp'=4] {'zl','y','core'}, dimensions={0} | all-to-all | bytes 98304 | tf_op jit(solution)/shard_map/all_to_all | solution.py:156
  (114 shorter events, 24.8 us)
Async XLA Ops:
  7.2 88.2 %copy-start = (bf16[768,256]{1,0:T(8,128)(2,1)S(1)}, bf16[768,256]{1,0:T(8,128)(2,1)}, u32[]{:S(2)}) copy-start(bf16[768,256]{1,0:T(8,128)(2,1)} %param.16) | copy-start | bytes 1179652
  7.2 79.3 %all-gather.5.cloned.1.call-start = ((), (), s32[]{:S(2)}) async-start(), calls=%async_computation.5 | async-start | bytes 5242880 | tf_op jit(solution)/shard_map/all_gather | solution.py:181
  9.7 10.7 %collective-permute-start = (bf16[3,32,768]{2,1,0:T(8,128)(2,1)S(1)}, bf16[3,32,768]{2,1,0:T(8,128)(2,1)S(1)}, u32[]{:S(2)}, u32[]{:S(2)}) collective-permute-start(bf16[3,32,768]{2,1,0:T(8,128)(2,1)S(1)} %get-tuple-element.88), channel_id=1, source_target_pairs={{0,4},{4,8},{8,12},{12,16},{16,20},{20,24},{24,28},{28,32},{32,36}... | collective-permute-start | bytes 442376 | tf_op jit(solution)/shard_map/ppermute | solution.py:23
  14.4 6.5 %collective-permute-start.1 = (bf16[3,32,768]{2,1,0:T(8,128)(2,1)S(1)}, bf16[3,32,768]{2,1,0:T(8,128)(2,1)S(1)}, u32[]{:S(2)}, u32[]{:S(2)}) collective-permute-start(bf16[3,32,768]{2,1,0:T(8,128)(2,1)S(1)} %get-tuple-element.89), channel_id=1, source_target_pairs={{4,0},{8,4},{12,8},{16,12},{20,16},{24,20},{28,24},{32,28},{36,32}... | collective-permute-start | bytes 442376 | tf_op jit(solution)/shard_map/ppermute | solution.py:24
  21.1 37.6 %copy-start.12 = (f32[768]{0:T(1024)S(1)}, f32[768]{0:T(1024)}, u32[]{:S(2)}) copy-start(f32[768]{0:T(1024)} %param.14) | copy-start | bytes 9220
  21.1 37.6 %copy-start.13 = (f32[768]{0:T(1024)S(1)}, f32[768]{0:T(1024)}, u32[]{:S(2)}) copy-start(f32[768]{0:T(1024)} %param.13) | copy-start | bytes 9220
  21.1 37.6 %copy-start.14 = (f32[768]{0:T(1024)S(1)}, f32[768]{0:T(1024)}, u32[]{:S(2)}) copy-start(f32[768]{0:T(1024)} %param.15) | copy-start | bytes 9220
  26.3 32.7 %all-to-all-start = ((bf16[4,128,256]{2,1,0:T(8,128)(2,1)}), bf16[4,128,256]{2,1,0:T(8,128)(2,1)S(1)}, u32[]{:S(2)}, u32[]{:S(2)}) async-start(bf16[4,128,256]{2,1,0:T(8,128)(2,1)} %broadcast_in_dim.110), calls=%async_computation | async-start | bytes 524288 | tf_op jit(solution)/shard_map/all_to_all | solution.py:156
  41.1 31.7 %copy-start.15 = (s32[1,256]{1,0:T(1,128)S(1)}, s32[1,256]{1,0:T(1,128)}, u32[]{:S(2)}) copy-start(s32[1,256]{1,0:T(1,128)} %param.18) | copy-start | bytes 3076
  59.0 29.7 %copy-start.10 = (bf16[8,768]{1,0:T(8,128)(2,1)}, bf16[8,768]{1,0:T(8,128)(2,1)S(1)}, u32[]{:S(2)}) copy-start(bf16[8,768]{1,0:T(8,128)(2,1)S(1)} %multiply_convert_fusion) | copy-start | bytes 36868
  59.8 26.7 %all-to-all-start.1 = ((bf16[32,8,768]{2,1,0:T(8,128)(2,1)}), bf16[32,8,768]{2,1,0:T(8,128)(2,1)S(1)}, u32[]{:S(2)}, u32[]{:S(2)}) async-start(bf16[32,8,768]{2,1,0:T(8,128)(2,1)} %broadcast_in_dim.120), calls=%async_computation.1 | async-start | bytes 786432 | tf_op jit(solution)/shard_map/all_to_all | solution.py:156
  72.7 110.7 %all-gather.7.cloned.1.call-start = ((), (), s32[]{:S(2)}) async-start(), calls=%async_computation.6 | async-start | bytes 4325376 | tf_op jit(solution)/shard_map/all_gather | solution.py:239
  88.9 35.2 %copy-start.1 = (bf16[256,2048]{1,0:T(8,128)(2,1)}, bf16[256,2048]{1,0:T(8,128)(2,1)S(1)}, u32[]{:S(2)}) copy-start(bf16[256,2048]{1,0:T(8,128)(2,1)S(1)} %pad.9.refs_3_) | copy-start | bytes 3145732
  88.9 35.3 %collective-permute-start.6 = (bf16[256,2048]{1,0:T(8,128)(2,1)S(1)}, bf16[256,2048]{1,0:T(8,128)(2,1)S(1)}, u32[]{:S(2)}, u32[]{:S(2)}) collective-permute-start(bf16[256,2048]{1,0:T(8,128)(2,1)S(1)} %pad.9.refs_3_), channel_id=1, source_target_pairs={{3,0},{0,1},{1,2},{2,3},{7,4},{4,5},{5,6},{6,7},{11,8},{8,9},{9,10... | collective-permute-start | bytes 3145736 | tf_op jit(solution)/shard_map/ppermute | solution.py:16
  92.0 32.2 %collective-permute-start.7 = (bf16[256,2048]{1,0:T(8,128)(2,1)S(1)}, bf16[256,2048]{1,0:T(8,128)(2,1)}, u32[]{:S(2)}, u32[]{:S(2)}) collective-permute-start(bf16[256,2048]{1,0:T(8,128)(2,1)S(1)} %pad.9.refs_3_), channel_id=1, source_target_pairs={{1,0},{2,1},{3,2},{0,3},{5,4},{6,5},{7,6},{4,7},{9,8},{10,9},{11,1... | collective-permute-start | bytes 3145736 | tf_op jit(solution)/shard_map/ppermute | solution.py:16
  95.7 13.4 %collective-permute-start.2 = (bf16[128,256]{1,0:T(8,128)(2,1)S(1)}, bf16[128,256]{1,0:T(8,128)(2,1)S(1)}, u32[]{:S(2)}, u32[]{:S(2)}) collective-permute-start(bf16[128,256]{1,0:T(8,128)(2,1)S(1)} %get-tuple-element.86), channel_id=1, source_target_pairs={{0,128},{128,0},{256,384},{384,256},{1,129},{129,1},{257,385},{385... | collective-permute-start | bytes 196616 | tf_op jit(solution)/shard_map/ppermute | solution.py:151
  97.6 12.7 %collective-permute-start.4 = (bf16[128,256]{1,0:T(8,128)(2,1)S(1)}, bf16[128,256]{1,0:T(8,128)(2,1)S(1)}, u32[]{:S(2)}, u32[]{:S(2)}) collective-permute-start(bf16[128,256]{1,0:T(8,128)(2,1)S(1)} %get-tuple-element.87), channel_id=1, source_target_pairs={{0,384},{128,256},{256,128},{384,0},{1,385},{129,257},{257,129},{3... | collective-permute-start | bytes 196616 | tf_op jit(solution)/shard_map/ppermute | solution.py:151
  110.4 9.7 %collective-permute-start.3 = (bf16[128,256]{1,0:T(8,128)(2,1)S(1)}, bf16[128,256]{1,0:T(8,128)(2,1)S(1)}, u32[]{:S(2)}, u32[]{:S(2)}) collective-permute-start(bf16[128,256]{1,0:T(8,128)(2,1)S(1)} %get-tuple-element.84), channel_id=1, source_target_pairs={{0,384},{128,256},{256,128},{384,0},{1,385},{129,257},{257,129},{3... | collective-permute-start | bytes 196616 | tf_op jit(solution)/shard_map/ppermute | solution.py:151
  114.6 9.5 %collective-permute-start.5 = (bf16[128,256]{1,0:T(8,128)(2,1)S(1)}, bf16[128,256]{1,0:T(8,128)(2,1)S(1)}, u32[]{:S(2)}, u32[]{:S(2)}) collective-permute-start(bf16[128,256]{1,0:T(8,128)(2,1)S(1)} %get-tuple-element.85), channel_id=1, source_target_pairs={{0,128},{128,0},{256,384},{384,256},{1,129},{129,1},{257,385},{385... | collective-permute-start | bytes 196616 | tf_op jit(solution)/shard_map/ppermute | solution.py:151
  124.2 34.0 %copy-start.3 = (bf16[256,2048]{1,0:T(8,128)(2,1)}, bf16[256,2048]{1,0:T(8,128)(2,1)S(1)}, u32[]{:S(2)}) copy-start(bf16[256,2048]{1,0:T(8,128)(2,1)S(1)} %collective-permute-done.6.refs_4_) | copy-start | bytes 3145732
  154.6 28.8 %all-to-all-start.3 = ((bf16[4,4,256,256]{3,2,1,0:T(8,128)(2,1)}), bf16[4,4,256,256]{3,2,1,0:T(8,128)(2,1)S(1)}, u32[]{:S(2)}, u32[]{:S(2)}) async-start(bf16[4,4,256,256]{3,2,1,0:T(8,128)(2,1)} %broadcast_in_dim.122), calls=%async_computation.3 | async-start | bytes 4194304 | tf_op jit(solution)/shard_map/all_to_all | solution.py:156
  158.3 15.4 %collective-permute-start.8 = (bf16[128,2048]{1,0:T(8,128)(2,1)S(1)}, bf16[128,2048]{1,0:T(8,128)(2,1)S(1)}, u32[]{:S(2)}, u32[]{:S(2)}) collective-permute-start(bf16[128,2048]{1,0:T(8,128)(2,1)S(1)} %slice.459), channel_id=1, source_target_pairs={{3,0},{0,1},{1,2},{2,3},{7,4},{4,5},{5,6},{6,7},{11,8},{8,9},{9,10... | collective-permute-start | bytes 1572872 | tf_op jit(solution)/shard_map/ppermute | solution.py:16
  161.4 14.3 %collective-permute-start.9 = (bf16[128,2048]{1,0:T(8,128)(2,1)S(1)}, bf16[128,2048]{1,0:T(8,128)(2,1)S(1)}, u32[]{:S(2)}, u32[]{:S(2)}) collective-permute-start(bf16[128,2048]{1,0:T(8,128)(2,1)S(1)} %slice.460), channel_id=1, source_target_pairs={{1,0},{2,1},{3,2},{0,3},{5,4},{6,5},{7,6},{4,7},{9,8},{10,9},{11,1... | collective-permute-start | bytes 1572872 | tf_op jit(solution)/shard_map/ppermute | solution.py:16
  183.4 16.2 %collective-permute-start.10 = (bf16[4,4,256,256]{3,2,1,0:T(8,128)(2,1)S(1)}, bf16[4,4,256,256]{3,2,1,0:T(8,128)(2,1)}, u32[]{:S(2)}, u32[]{:S(2)}) collective-permute-start(bf16[4,4,256,256]{3,2,1,0:T(8,128)(2,1)S(1)} %all-to-all-done.3.refs_0_), channel_id=1, source_target_pairs={{0,4},{4,0},{1,5},{5,1},{2,6},{6,2},{3,7},{7,3},{8,12},{12,8},{9,1... | collective-permute-start | bytes 6291464 | tf_op jit(solution)/shard_map/ppermute | solution.py:249
  (13 other events, 193.4 us)
Sparse Core Ops, SparseCore 0:
  10.1 61.2 all-gather.4
  87.6 69.9 all-gather.6

commit v2 on v1

--- a/solution.py
+++ b/solution.py
@@ -182,13 +182,12 @@
     high = jnp.pad(weight[WIDE:], ((0, 2 * WIDE - columns), (0, 0)))
     left, right = shifted(high, "dp", -1), shifted(high, "dp", 1)
 
+    text = to_all(text_embed[0], "section")
+
     image = features[0]
     height, width, chans = image.shape
     above, below = extended(image, VOCAB, 3)
     padded = jnp.concatenate([above, image, below])
-
-    text, _, _ = lax.optimization_barrier((text_embed[0], above, below))
-    text = to_all(text, "section")
 
     padded = jnp.pad(padded, ((0, 0), (3, 3), (0, 0))).astype(jnp.float32)
     conv = jnp.zeros((height, width, chans), jnp.float32)
@@ -202,6 +201,7 @@
     sums = jnp.stack(
         [jnp.sum(conv, axis=-1).reshape(-1), jnp.sum(conv * conv, axis=-1).reshape(-1)]
     )
+    sums, text = lax.optimization_barrier((sums, text))
     sums = lax.psum(sums, "section")
     all_chans = chans * sections
     middle = sums[0].reshape(height, width) / all_chans
@@ -211,17 +211,11 @@
     pooled = block.reshape(height // 4, 4, width // 4, 4, chans).mean(axis=(1, 3))
     pooled = pooled.reshape(-1, chans).astype(jnp.bfloat16)
 
-    pooled, text = lax.optimization_barrier((pooled, text))
     tokens = to_all(pooled, VOCAB)
     rows = jnp.dot(tokens.reshape(-1, chans), proj_weight, preferred_element_type=jnp.float32)
-    middle_row = rows.shape[0] // 2
-    halves = [rows[:middle_row], rows[middle_row:]]
-    for step in range(2):
-        halves = [
-            half + across(half.astype(jnp.bfloat16), step ^ at).astype(jnp.float32)
-            for at, half in enumerate(halves)
-        ]
-    rows = jnp.concatenate([half.astype(jnp.bfloat16) for half in halves])
+    for turn in range(2):
+        rows = rows + across(rows.astype(jnp.bfloat16), turn).astype(jnp.float32)
+    rows = rows.astype(jnp.bfloat16)
 
     is_text = jnp.all(slots[:, None] != places[None, :], axis=1)
     rank = jnp.sum(
@@ -278,11 +272,10 @@
             [top, jnp.sum(totals * jnp.exp(tops - top), axis=0), jnp.sum(chosen, axis=0)]
         )
 
-    section = lax.axis_index("section")
-    mine = lax.iota(jnp.int32, sections)[:, None, None] == section
-    both = lax.psum(jnp.where(mine, both[None], 0.0), "section")
-    both = both.reshape(sections, 3, sections, -1)
-    both = merged(lax.dynamic_index_in_dim(both, section, 2, keepdims=False))
+    for turn in range(2):
+        both = merged(jnp.stack([both, across(both, turn)]))
+    both = both.reshape(3, sections, -1)
+    both = lax.dynamic_index_in_dim(both, lax.axis_index("section"), 1, keepdims=False)
     top, total, chosen = merged(to_all(both, VOCAB))
     loss = top + jnp.log(total) - chosen
     return (pooled[None], loss[None])

time: 250 us -> 249 us (level)
  blocking collectives: 77.6 us -> 34.5 us
  waiting for transfers between devices: 43.7 us -> 76.2 us
  starting transfers between devices: 74.8 us -> 83 us
    all_to_all x2 -> x1, blocking collectives: 43.8 us -> 21.2 us  [to_all(): lax.all_to_all(jnp.broadcast_to(value[None], (count,) + value.shape), axi...]
    all_to_all x3 -> x4, waiting for transfers between devices: 21.1 us -> 37.6 us  [to_all(): lax.all_to_all(jnp.broadcast_to(value[None], (count,) + value.shape), axi...]
    psum x1 -> x0, blocking collectives: 16.4 us -> none  [shards(): both = lax.psum(jnp.where(mine, both[None], 0.0), 'section')]
    ppermute x4, waiting for transfers between devices: 12.2 us -> 28.6 us  [across(): return lax.ppermute(value, 'section', pairs)]
    ppermute x4, starting transfers between devices: 16.1 us -> 20.3 us  [across(): return lax.ppermute(value, 'section', pairs)]
    psum x1, blocking collectives: 17.4 us -> 13.2 us  [shards(): sums = lax.psum(sums, 'section')]
    ppermute x4, starting transfers between devices: 13 us -> 16.2 us  [shifted(): lax.ppermute(value, axis, [((i + step) % count, i) for i in range(count)])]
    all_to_all x3 -> x4, starting transfers between devices: 31.3 us -> 31.1 us  [to_all(): lax.all_to_all(jnp.broadcast_to(value[None], (count,) + value.shape), axi...]
  transfers between devices with their start and end apart: 16 -> 17, of which waited for: 9 -> 10; matrix products, arithmetic and copies ran while one was open for 6% -> 6% of each run, Pallas kernels for 4% -> 4%
where the time goes in v2:
time: 249 us; the launch traced here: 247 us
  starting transfers between devices  83 us (33%)
  waiting for transfers between devices  76.2 us (31%)
  blocking collectives  34.5 us (14%)
  Pallas kernels  17.5 us (7%)
  between operations  14.6 us (6%)
  local copies, waits for them, and re-layouts  12 us (5%)
  other arithmetic  8.29 us (3%)
    all_to_all x4, waiting for transfers between devices, to_all(): lax.all_to_all(jnp.broadcast_to(value[None], (count,) + value.shape), axi...  37.6 us
    all_to_all x4, starting transfers between devices, to_all(): lax.all_to_all(jnp.broadcast_to(value[None], (count,) + value.shape), axi...  31.1 us
    ppermute x4, waiting for transfers between devices, across(): return lax.ppermute(value, 'section', pairs)  28.6 us
    all_to_all x1, blocking collectives, to_all(): lax.all_to_all(jnp.broadcast_to(value[None], (count,) + value.shape), axi...  21.2 us
    ppermute x4, starting transfers between devices, across(): return lax.ppermute(value, 'section', pairs)  20.3 us
    pallas_call x2, Pallas kernels, head_stats(): pl.pallas_call(functools.partial(head_kernel, columns, offsets, from_text...  17.5 us
    ppermute x4, starting transfers between devices, shifted(): lax.ppermute(value, axis, [((i + step) % count, i) for i in range(count)])  16.2 us
    psum x1, blocking collectives, shards(): sums = lax.psum(sums, 'section')  13.2 us
  transfers between devices with their start and end apart: 17, of which 10 were waited for; matrix products, arithmetic and copies ran while one was open for 6% of the time, Pallas kernels for 4%

profile of v2, /device:TPU:1, one launch (start us, length us, event | category | flops | bytes accessed | tf_op | source)
XLA Modules:
  0.0 247.2 jit_solution(3900140581847114609)
XLA Ops:
  9.7 4.7 %collective-permute-start = (bf16[3,32,768]{2,1,0:T(8,128)(2,1)S(1)}, bf16[3,32,768]{2,1,0:T(8,128)(2,1)S(1)}, u32[]{:S(2)}, u32[]{:S(2)}) collective-permute-start(bf16[3,32,768]{2,1,0:T(8,128)(2,1)S(1)} %get-tuple-element.82), channel_id=1, source_target_pairs={{0,4},{4,8},{8,12},{12,16},{16,20},{20,24},{24,28},{28,32},{32,36}... | collective-permute-start | bytes 442376 | tf_op jit(solution)/shard_map/ppermute | solution.py:23
  14.4 5.5 %collective-permute-start.1 = (bf16[3,32,768]{2,1,0:T(8,128)(2,1)S(1)}, bf16[3,32,768]{2,1,0:T(8,128)(2,1)S(1)}, u32[]{:S(2)}, u32[]{:S(2)}) collective-permute-start(bf16[3,32,768]{2,1,0:T(8,128)(2,1)S(1)} %get-tuple-element.83), channel_id=1, source_target_pairs={{4,0},{8,4},{12,8},{16,12},{20,16},{24,20},{28,24},{32,28},{36,32}... | collective-permute-start | bytes 442376 | tf_op jit(solution)/shard_map/ppermute | solution.py:24
  20.6 11.2 %all-to-all-start = ((bf16[4,128,256]{2,1,0:T(8,128)(2,1)}), bf16[4,128,256]{2,1,0:T(8,128)(2,1)S(1)}, u32[]{:S(2)}, u32[]{:S(2)}) async-start(bf16[4,128,256]{2,1,0:T(8,128)(2,1)} %broadcast_in_dim.51), calls=%async_computation | async-start | bytes 524288 | tf_op jit(solution)/shard_map/all_to_all | solution.py:156
  32.5 4.3 %fusion.79 = (f32[4,32]{1,0:T(4,128)S(1)}, f32[4,32]{1,0:T(4,128)S(1)}, f32[4,32,768]{2,1,0:T(8,128)S(1)}) fusion(f32[768]{0:T(1024)S(1)} %get-tuple-element.71, f32[10,38,768]{2,1,0:T(8,128)S(1)} %fusion.7, f32[768]{0:T(1024)S(1)} %get-tuple-element.72, f32[768]{0:T(1024)S(1)} %get-tuple-element.25, f32[768]{0:T(1024)S(1)} %get-tuple-element.26, ...), kind=kLoop, calls=%fused_computation.221 | loop fusion | flops 9830144 | bytes 19812352 | tf_op jit(solution)/shard_map/reduce_sum | solution.py:202
  37.0 12.7 %all-to-all-done = bf16[4,128,256]{2,1,0:T(8,128)(2,1)S(1)} async-done(((bf16[4,128,256]{2,1,0:T(8,128)(2,1)}), bf16[4,128,256]{2,1,0:T(8,128)(2,1)S(1)}, u32[]{:S(2)}, u32[]{:S(2)}) %all-to-all-start) | async-done | bytes 262176 | tf_op jit(solution)/shard_map/all_to_all | solution.py:156
  49.7 13.2 %psum.7 = f32[2,128]{1,0:T(2,128)S(1)} all-reduce(f32[2,128]{1,0:T(2,128)S(1)} %pad_maximum_fusion.5), channel_id=1, replica_groups=mesh['section'=4,'zl'=4,'y'=4,'core'=2,'dp'=4] {'section'}, use_global_device_ids=true, to_apply=%region_2.3 | all-reduce | flops 256 | bytes 2048 | tf_op jit(solution)/shard_map/psum | solution.py:205
  64.3 8.9 %all-to-all-start.1 = ((bf16[32,8,768]{2,1,0:T(8,128)(2,1)}), bf16[32,8,768]{2,1,0:T(8,128)(2,1)S(1)}, u32[]{:S(2)}, u32[]{:S(2)}) async-start(bf16[32,8,768]{2,1,0:T(8,128)(2,1)} %broadcast_in_dim.99), calls=%async_computation.1 | async-start | bytes 786432 | tf_op jit(solution)/shard_map/all_to_all | solution.py:156
  73.5 13.4 %all-to-all-done.1 = bf16[32,8,768]{2,1,0:T(8,128)(2,1)S(1)} async-done(((bf16[32,8,768]{2,1,0:T(8,128)(2,1)}), bf16[32,8,768]{2,1,0:T(8,128)(2,1)S(1)}, u32[]{:S(2)}, u32[]{:S(2)}) %all-to-all-start.1) | async-done | bytes 393248 | tf_op jit(solution)/shard_map/all_to_all | solution.py:156
  96.1 5.2 %collective-permute-start.2 = (bf16[256,256]{1,0:T(8,128)(2,1)S(1)}, bf16[256,256]{1,0:T(8,128)(2,1)S(1)}, u32[]{:S(2)}, u32[]{:S(2)}) collective-permute-start(bf16[256,256]{1,0:T(8,128)(2,1)S(1)} %get-tuple-element.92), channel_id=1, source_target_pairs={{0,128},{128,0},{256,384},{384,256},{1,129},{129,1},{257,385},{385... | collective-permute-start | bytes 393224 | tf_op jit(solution)/shard_map/ppermute | solution.py:151
  101.2 13.7 %collective-permute-done.2 = bf16[256,256]{1,0:T(8,128)(2,1)S(1)} collective-permute-done((bf16[256,256]{1,0:T(8,128)(2,1)S(1)}, bf16[256,256]{1,0:T(8,128)(2,1)S(1)}, u32[]{:S(2)}, u32[]{:S(2)}) %collective-permute-start.2) | collective-permute-done | bytes 131104 | tf_op jit(solution)/shard_map/ppermute | solution.py:151
  116.9 11.5 %collective-permute-done.3 = bf16[256,256]{1,0:T(8,128)(2,1)S(1)} collective-permute-done((bf16[256,256]{1,0:T(8,128)(2,1)S(1)}, bf16[256,256]{1,0:T(8,128)(2,1)S(1)}, u32[]{:S(2)}, u32[]{:S(2)}) %collective-permute-start.3) | collective-permute-done | bytes 131104 | tf_op jit(solution)/shard_map/ppermute | solution.py:151
  128.6 21.2 %all_to_all.25.refs_1_ = bf16[4,256,256]{2,1,0:T(8,128)(2,1)S(1)} all-to-all(bf16[4,256,256]{2,1,0:T(8,128)(2,1)S(1)} %broadcast_in_dim.100), channel_id=1, replica_groups=mesh['section'=4,'zl'=4,'y'=4,'core'=2,'dp'=4] {'zl'}, dimensions={0} | all-to-all | bytes 1048576 | tf_op jit(solution)/shard_map/all_to_all | solution.py:156
  152.2 3.6 %all-to-all-start.3 = ((bf16[4,4,256,256]{3,2,1,0:T(8,128)(2,1)}), bf16[4,4,256,256]{3,2,1,0:T(8,128)(2,1)S(1)}, u32[]{:S(2)}, u32[]{:S(2)}) async-start(bf16[4,4,256,256]{3,2,1,0:T(8,128)(2,1)} %broadcast_in_dim.101), calls=%async_computation.3 | async-start | bytes 4194304 | tf_op jit(solution)/shard_map/all_to_all | solution.py:156
  155.9 5.8 %collective-permute-start.6 = (bf16[128,2048]{1,0:T(8,128)(2,1)S(1)}, bf16[128,2048]{1,0:T(8,128)(2,1)S(1)}, u32[]{:S(2)}, u32[]{:S(2)}) collective-permute-start(bf16[128,2048]{1,0:T(8,128)(2,1)S(1)} %slice.460), channel_id=1, source_target_pairs={{3,0},{0,1},{1,2},{2,3},{7,4},{4,5},{5,6},{6,7},{11,8},{8,9},{9,10... | collective-permute-start | bytes 1572872 | tf_op jit(solution)/shard_map/ppermute | solution.py:16
  162.7 3.9 %collective-permute-start.7 = (bf16[128,2048]{1,0:T(8,128)(2,1)S(1)}, bf16[128,2048]{1,0:T(8,128)(2,1)S(1)}, u32[]{:S(2)}, u32[]{:S(2)}) collective-permute-start(bf16[128,2048]{1,0:T(8,128)(2,1)S(1)} %slice.461), channel_id=1, source_target_pairs={{1,0},{2,1},{3,2},{0,3},{5,4},{6,5},{7,6},{4,7},{9,8},{10,9},{11,1... | collective-permute-start | bytes 1572872 | tf_op jit(solution)/shard_map/ppermute | solution.py:16
  166.7 8.0 %collective-permute-done.6.refs_6_ = bf16[128,2048]{1,0:T(8,128)(2,1)S(1)} collective-permute-done((bf16[128,2048]{1,0:T(8,128)(2,1)S(1)}, bf16[128,2048]{1,0:T(8,128)(2,1)S(1)}, u32[]{:S(2)}, u32[]{:S(2)}) %collective-permute-start.6) | collective-permute-done | bytes 524320 | tf_op jit(solution)/shard_map/ppermute | solution.py:16
  176.7 4.4 %all-to-all-done.3.refs_0_ = bf16[4,4,256,256]{3,2,1,0:T(8,128)(2,1)S(1)} async-done(((bf16[4,4,256,256]{3,2,1,0:T(8,128)(2,1)}), bf16[4,4,256,256]{3,2,1,0:T(8,128)(2,1)S(1)}, u32[]{:S(2)}, u32[]{:S(2)}) %all-to-all-start.3) | async-done | bytes 2097184 | tf_op jit(solution)/shard_map/all_to_all | solution.py:156
  181.1 5.1 %collective-permute-start.8 = (bf16[4,4,256,256]{3,2,1,0:T(8,128)(2,1)S(1)}, bf16[4,4,256,256]{3,2,1,0:T(8,128)(2,1)}, u32[]{:S(2)}, u32[]{:S(2)}) collective-permute-start(bf16[4,4,256,256]{3,2,1,0:T(8,128)(2,1)S(1)} %all-to-all-done.3.refs_0_), channel_id=1, source_target_pairs={{0,4},{4,0},{1,5},{5,1},{2,6},{6,2},{3,7},{7,3},{8,12},{12,8},{9,1... | collective-permute-start | bytes 6291464 | tf_op jit(solution)/shard_map/ppermute | solution.py:243
  188.9 9.2 %shard_map.122 = f32[8,512]{1,0:T(8,128)} custom-call(s32[2]{0:T(128)} %pad_add_fusion.2.own_ref, f32[32,1,256]{2,1,0:T(1,128)} %bitcast.81, s32[256,2]{1,0:T(8,128)} %copy.38.meta_ref, bf16[4,4,2,256,256]{4,3,2,1,0:T(8,128)(2,1)} %bitcast.74, bf16[4,256,256]{2,1,0:T(8,128)(2,1)} %copy-done.4, bf16[4,256,2048]{2,1,0:T(8,128)(2,1)} %bitcast.72, ...), custom_call_target="tpu_custom_call" | custom-call | flops 2147483648 | bytes 12582912 | tf_op jit(solution)/shard_map/pallas_call | solution.py:124
  198.2 8.3 %shard_map.123 = f32[8,512]{1,0:T(8,128)} custom-call(s32[2]{0:T(128)} %pad_add_fusion.2.own_ref, f32[32,1,256]{2,1,0:T(1,128)} %bitcast.82, s32[256,2]{1,0:T(8,128)} %copy.39.meta_ref, bf16[4,4,256,256]{3,2,1,0:T(8,128)(2,1)} %copy-done.2, bf16[4,4,256,256]{3,2,1,0:T(8,128)(2,1)} %collective-permute-done.8.refs_1_, bf16[4,256,2048]{2,1,0:T(8,128)(2,1)} %bitcast.73, ...), custom_call_target="tpu_custom_call" | custom-call | flops 2147483648 | bytes 12582912 | tf_op jit(solution)/shard_map/pallas_call | solution.py:124
  207.2 6.5 %collective-permute-start.9 = (f32[3,512]{1,0:T(4,128)S(1)}, f32[3,512]{1,0:T(4,128)S(1)}, u32[]{:S(2)}, u32[]{:S(2)}) collective-permute-start(f32[3,512]{1,0:T(4,128)S(1)} %slice_add_fusion), channel_id=1, source_target_pairs={{0,128},{128,0},{256,384},{384,256},{1,129},{129,1},{257,385},{385... | collective-permute-start | bytes 18440 | tf_op jit(solution)/shard_map/ppermute | solution.py:151
  215.6 6.8 %collective-permute-start.10 = (f32[3,512]{1,0:T(4,128)S(1)}, f32[3,512]{1,0:T(4,128)S(1)}, u32[]{:S(2)}, u32[]{:S(2)}) collective-permute-start(f32[3,512]{1,0:T(4,128)S(1)} %get-tuple-element.91), channel_id=1, source_target_pairs={{0,384},{128,256},{256,128},{384,0},{1,385},{129,257},{257,129},{3... | collective-permute-start | bytes 18440 | tf_op jit(solution)/shard_map/ppermute | solution.py:151
  224.7 7.3 %all-to-all-start.4 = ((f32[32,3,128]{2,1,0:T(4,128)}), f32[32,3,128]{2,1,0:T(4,128)S(1)}, u32[]{:S(2)}, u32[]{:S(2)}) async-start(f32[32,3,128]{2,1,0:T(4,128)} %broadcast_in_dim.104), calls=%async_computation.4 | async-start | bytes 131072 | tf_op jit(solution)/shard_map/all_to_all | solution.py:156
  232.6 7.1 %all-to-all-done.4 = f32[32,3,128]{2,1,0:T(4,128)S(1)} async-done(((f32[32,3,128]{2,1,0:T(4,128)}), f32[32,3,128]{2,1,0:T(4,128)S(1)}, u32[]{:S(2)}, u32[]{:S(2)}) %all-to-all-start.4) | async-done | bytes 49184 | tf_op jit(solution)/shard_map/all_to_all | solution.py:156
  (108 shorter events, 31.0 us)
Async XLA Ops:
  7.2 88.6 %copy-start = (bf16[768,256]{1,0:T(8,128)(2,1)S(1)}, bf16[768,256]{1,0:T(8,128)(2,1)}, u32[]{:S(2)}) copy-start(bf16[768,256]{1,0:T(8,128)(2,1)} %param.16) | copy-start | bytes 1179652
  7.2 79.8 %all-gather.5.cloned.1.call-start = ((), (), s32[]{:S(2)}) async-start(), calls=%async_computation.5 | async-start | bytes 5242880 | tf_op jit(solution)/shard_map/all_gather | solution.py:181
  9.7 22.6 %collective-permute-start = (bf16[3,32,768]{2,1,0:T(8,128)(2,1)S(1)}, bf16[3,32,768]{2,1,0:T(8,128)(2,1)S(1)}, u32[]{:S(2)}, u32[]{:S(2)}) collective-permute-start(bf16[3,32,768]{2,1,0:T(8,128)(2,1)S(1)} %get-tuple-element.82), channel_id=1, source_target_pairs={{0,4},{4,8},{8,12},{12,16},{16,20},{20,24},{24,28},{28,32},{32,36}... | collective-permute-start | bytes 442376 | tf_op jit(solution)/shard_map/ppermute | solution.py:23
  14.4 17.9 %collective-permute-start.1 = (bf16[3,32,768]{2,1,0:T(8,128)(2,1)S(1)}, bf16[3,32,768]{2,1,0:T(8,128)(2,1)S(1)}, u32[]{:S(2)}, u32[]{:S(2)}) collective-permute-start(bf16[3,32,768]{2,1,0:T(8,128)(2,1)S(1)} %get-tuple-element.83), channel_id=1, source_target_pairs={{4,0},{8,4},{12,8},{16,12},{20,16},{24,20},{28,24},{32,28},{36,32}... | collective-permute-start | bytes 442376 | tf_op jit(solution)/shard_map/ppermute | solution.py:24
  20.6 29.0 %all-to-all-start = ((bf16[4,128,256]{2,1,0:T(8,128)(2,1)}), bf16[4,128,256]{2,1,0:T(8,128)(2,1)S(1)}, u32[]{:S(2)}, u32[]{:S(2)}) async-start(bf16[4,128,256]{2,1,0:T(8,128)(2,1)} %broadcast_in_dim.51), calls=%async_computation | async-start | bytes 524288 | tf_op jit(solution)/shard_map/all_to_all | solution.py:156
  32.5 30.6 %copy-start.13 = (f32[768]{0:T(1024)S(1)}, f32[768]{0:T(1024)}, u32[]{:S(2)}) copy-start(f32[768]{0:T(1024)} %param.14) | copy-start | bytes 9220
  32.5 30.6 %copy-start.14 = (f32[768]{0:T(1024)S(1)}, f32[768]{0:T(1024)}, u32[]{:S(2)}) copy-start(f32[768]{0:T(1024)} %param.13) | copy-start | bytes 9220
  32.5 30.6 %copy-start.15 = (f32[768]{0:T(1024)S(1)}, f32[768]{0:T(1024)}, u32[]{:S(2)}) copy-start(f32[768]{0:T(1024)} %param.15) | copy-start | bytes 9220
  36.8 36.4 %copy-start.16 = (s32[1,256]{1,0:T(1,128)S(1)}, s32[1,256]{1,0:T(1,128)}, u32[]{:S(2)}) copy-start(s32[1,256]{1,0:T(1,128)} %param.18) | copy-start | bytes 3076
  64.3 22.7 %all-to-all-start.1 = ((bf16[32,8,768]{2,1,0:T(8,128)(2,1)}), bf16[32,8,768]{2,1,0:T(8,128)(2,1)S(1)}, u32[]{:S(2)}, u32[]{:S(2)}) async-start(bf16[32,8,768]{2,1,0:T(8,128)(2,1)} %broadcast_in_dim.99), calls=%async_computation.1 | async-start | bytes 786432 | tf_op jit(solution)/shard_map/all_to_all | solution.py:156
  73.2 107.9 %all-gather.7.cloned.1.call-start = ((), (), s32[]{:S(2)}) async-start(), calls=%async_computation.6 | async-start | bytes 4325376 | tf_op jit(solution)/shard_map/all_gather | solution.py:233
  89.3 39.3 %copy-start.1 = (bf16[256,2048]{1,0:T(8,128)(2,1)}, bf16[256,2048]{1,0:T(8,128)(2,1)S(1)}, u32[]{:S(2)}) copy-start(bf16[256,2048]{1,0:T(8,128)(2,1)S(1)} %pad.9.refs_3_) | copy-start | bytes 3145732
  89.3 39.2 %collective-permute-start.4 = (bf16[256,2048]{1,0:T(8,128)(2,1)S(1)}, bf16[256,2048]{1,0:T(8,128)(2,1)S(1)}, u32[]{:S(2)}, u32[]{:S(2)}) collective-permute-start(bf16[256,2048]{1,0:T(8,128)(2,1)S(1)} %pad.9.refs_3_), channel_id=1, source_target_pairs={{3,0},{0,1},{1,2},{2,3},{7,4},{4,5},{5,6},{6,7},{11,8},{8,9},{9,10... | collective-permute-start | bytes 3145736 | tf_op jit(solution)/shard_map/ppermute | solution.py:16
  92.4 36.1 %collective-permute-start.5 = (bf16[256,2048]{1,0:T(8,128)(2,1)S(1)}, bf16[256,2048]{1,0:T(8,128)(2,1)}, u32[]{:S(2)}, u32[]{:S(2)}) collective-permute-start(bf16[256,2048]{1,0:T(8,128)(2,1)S(1)} %pad.9.refs_3_), channel_id=1, source_target_pairs={{1,0},{2,1},{3,2},{0,3},{5,4},{6,5},{7,6},{4,7},{9,8},{10,9},{11,1... | collective-permute-start | bytes 3145736 | tf_op jit(solution)/shard_map/ppermute | solution.py:16
  96.1 18.9 %collective-permute-start.2 = (bf16[256,256]{1,0:T(8,128)(2,1)S(1)}, bf16[256,256]{1,0:T(8,128)(2,1)S(1)}, u32[]{:S(2)}, u32[]{:S(2)}) collective-permute-start(bf16[256,256]{1,0:T(8,128)(2,1)S(1)} %get-tuple-element.92), channel_id=1, source_target_pairs={{0,128},{128,0},{256,384},{384,256},{1,129},{129,1},{257,385},{385... | collective-permute-start | bytes 393224 | tf_op jit(solution)/shard_map/ppermute | solution.py:151
  115.0 13.5 %collective-permute-start.3 = (bf16[256,256]{1,0:T(8,128)(2,1)S(1)}, bf16[256,256]{1,0:T(8,128)(2,1)S(1)}, u32[]{:S(2)}, u32[]{:S(2)}) collective-permute-start(bf16[256,256]{1,0:T(8,128)(2,1)S(1)} %fusion.63), channel_id=1, source_target_pairs={{0,384},{128,256},{256,128},{384,0},{1,385},{129,257},{257,129},{3... | collective-permute-start | bytes 393224 | tf_op jit(solution)/shard_map/ppermute | solution.py:151
  152.2 28.9 %all-to-all-start.3 = ((bf16[4,4,256,256]{3,2,1,0:T(8,128)(2,1)}), bf16[4,4,256,256]{3,2,1,0:T(8,128)(2,1)S(1)}, u32[]{:S(2)}, u32[]{:S(2)}) async-start(bf16[4,4,256,256]{3,2,1,0:T(8,128)(2,1)} %broadcast_in_dim.101), calls=%async_computation.3 | async-start | bytes 4194304 | tf_op jit(solution)/shard_map/all_to_all | solution.py:156
  155.9 18.8 %collective-permute-start.6 = (bf16[128,2048]{1,0:T(8,128)(2,1)S(1)}, bf16[128,2048]{1,0:T(8,128)(2,1)S(1)}, u32[]{:S(2)}, u32[]{:S(2)}) collective-permute-start(bf16[128,2048]{1,0:T(8,128)(2,1)S(1)} %slice.460), channel_id=1, source_target_pairs={{3,0},{0,1},{1,2},{2,3},{7,4},{4,5},{5,6},{6,7},{11,8},{8,9},{9,10... | collective-permute-start | bytes 1572872 | tf_op jit(solution)/shard_map/ppermute | solution.py:16
  162.7 13.9 %collective-permute-start.7 = (bf16[128,2048]{1,0:T(8,128)(2,1)S(1)}, bf16[128,2048]{1,0:T(8,128)(2,1)S(1)}, u32[]{:S(2)}, u32[]{:S(2)}) collective-permute-start(bf16[128,2048]{1,0:T(8,128)(2,1)S(1)} %slice.461), channel_id=1, source_target_pairs={{1,0},{2,1},{3,2},{0,3},{5,4},{6,5},{7,6},{4,7},{9,8},{10,9},{11,1... | collective-permute-start | bytes 1572872 | tf_op jit(solution)/shard_map/ppermute | solution.py:16
  181.1 17.1 %collective-permute-start.8 = (bf16[4,4,256,256]{3,2,1,0:T(8,128)(2,1)S(1)}, bf16[4,4,256,256]{3,2,1,0:T(8,128)(2,1)}, u32[]{:S(2)}, u32[]{:S(2)}) collective-permute-start(bf16[4,4,256,256]{3,2,1,0:T(8,128)(2,1)S(1)} %all-to-all-done.3.refs_0_), channel_id=1, source_target_pairs={{0,4},{4,0},{1,5},{5,1},{2,6},{6,2},{3,7},{7,3},{8,12},{12,8},{9,1... | collective-permute-start | bytes 6291464 | tf_op jit(solution)/shard_map/ppermute | solution.py:243
  198.2 33.8 %copy-start.9 = (f32[8,768]{1,0:T(8,128)S(1)}, f32[8,768]{1,0:T(8,128)}, u32[]{:S(2)}) copy-start(f32[8,768]{1,0:T(8,128)} %copy-done.8) | copy-start | bytes 73732
  207.2 8.3 %collective-permute-start.9 = (f32[3,512]{1,0:T(4,128)S(1)}, f32[3,512]{1,0:T(4,128)S(1)}, u32[]{:S(2)}, u32[]{:S(2)}) collective-permute-start(f32[3,512]{1,0:T(4,128)S(1)} %slice_add_fusion), channel_id=1, source_target_pairs={{0,128},{128,0},{256,384},{384,256},{1,129},{129,1},{257,385},{385... | collective-permute-start | bytes 18440 | tf_op jit(solution)/shard_map/ppermute | solution.py:151
  215.6 8.3 %collective-permute-start.10 = (f32[3,512]{1,0:T(4,128)S(1)}, f32[3,512]{1,0:T(4,128)S(1)}, u32[]{:S(2)}, u32[]{:S(2)}) collective-permute-start(f32[3,512]{1,0:T(4,128)S(1)} %get-tuple-element.91), channel_id=1, source_target_pairs={{0,384},{128,256},{256,128},{384,0},{1,385},{129,257},{257,129},{3... | collective-permute-start | bytes 18440 | tf_op jit(solution)/shard_map/ppermute | solution.py:151
  224.7 15.1 %all-to-all-start.4 = ((f32[32,3,128]{2,1,0:T(4,128)}), f32[32,3,128]{2,1,0:T(4,128)S(1)}, u32[]{:S(2)}, u32[]{:S(2)}) async-start(f32[32,3,128]{2,1,0:T(4,128)} %broadcast_in_dim.104), calls=%async_computation.4 | async-start | bytes 131072 | tf_op jit(solution)/shard_map/all_to_all | solution.py:156
  (11 other events, 146.4 us)
Sparse Core Ops, SparseCore 0:
  10.1 61.2 all-gather.4
  88.0 78.3 all-gather.6
